TPU v7x, 32 devices: a whole 2x2x4 slice. The times are simulated.
32 devices in a mesh: src: 8 (over y, x, core), rcv: 4 (over z).
Axes of the slice: x: 2, y: 2, z: 4, core: 2. Of those that a mesh axis runs over, the one named last changes fastest.
Arguments:
- recorded: bfloat16 [2, 16384, 16384], P(None, 'src', 'rcv'), may hold values from -6 to 6
- obliquity: float32 [4, 4096], replicated, may hold values from 0.01 to 0.25
- clip_level: float32 [16384], P('src'), may hold values from 0.3 to 3
Outputs:
- first_pass: bfloat16 [2, 16384, 16384], P(None, 'src', 'rcv')
- primaries: bfloat16 [2, 16384, 16384], P(None, 'src', 'rcv')
All inputs are finite; a program needn't handle non-finite values.
Results may differ from a plain program's by a relative error of at most 0.0025.
Values may be sent and summed in bfloat16 or wider, within the bound.
No kernel may reach another device: no remote copies, remote signals or barrier semaphores. Data moves between devices by JAX's collectives and lax.ppermute only.
A program may use at most 576 MiB of HBM per device.

v0:
```python
import math

import jax
import jax.numpy as jnp
from jax import lax
from jax.sharding import PartitionSpec as P

N = 16384
K = 256


TWO_PI = 2.0 * math.pi


def rotate(real_part, imag_part, cosine, sine_part):
    return (real_part * cosine - imag_part * sine_part, real_part * sine_part + imag_part * cosine)


def twiddle(real_part, imag_part, column_index, group_index, orient, total_length):
    angles = (column_index * group_index % total_length).astype(jnp.float32) * (
        TWO_PI / total_length
    )
    return rotate(real_part, imag_part, jnp.cos(angles), orient * jnp.sin(angles))


def long_table(length, orient):
    index_left = lax.broadcasted_iota(jnp.int32, (length, length), 0)
    index_right = lax.broadcasted_iota(jnp.int32, (length, length), 1)
    angles = (index_left * index_right % length).astype(jnp.float32) * (TWO_PI / length)
    cosine = jnp.cos(angles)
    sine_part = orient * jnp.sin(angles)
    upper = jnp.concatenate([cosine, sine_part], axis=1)
    lower = jnp.concatenate([-sine_part, cosine], axis=1)
    return jnp.concatenate([upper, lower], axis=0)


def long_transform(real_part, imag_part, orient):
    length = real_part.shape[-1]
    joined = jnp.concatenate([real_part, imag_part], axis=-1)
    result = jnp.dot(
        joined.reshape(-1, 2 * length),
        long_table(length, orient),
        precision=lax.Precision.HIGHEST,
        preferred_element_type=jnp.float32,
    )
    result = result.reshape(joined.shape)
    return (result[..., :length], result[..., length:])


def across_groups(real_part, imag_part, groups, orient):
    index_left = lax.broadcasted_iota(jnp.int32, (groups, groups), 0)
    index_right = lax.broadcasted_iota(jnp.int32, (groups, groups), 1)
    angles = (index_left * index_right % groups).astype(jnp.float32) * (TWO_PI / groups)
    cosine = jnp.cos(angles)
    sine_part = orient * jnp.sin(angles)
    highest = lax.Precision.HIGHEST
    new_real = jnp.einsum("mgc,gk->mkc", real_part, cosine, precision=highest) - jnp.einsum(
        "mgc,gk->mkc", imag_part, sine_part, precision=highest
    )
    new_imag = jnp.einsum("mgc,gk->mkc", real_part, sine_part, precision=highest) + jnp.einsum(
        "mgc,gk->mkc", imag_part, cosine, precision=highest
    )
    return (new_real, new_imag)


def filter_rows(whole_rows, obliquity, groups):
    row_total = whole_rows.shape[1]
    group_cols = whole_rows.shape[2] // groups
    total_length = groups * group_cols
    values = whole_rows.astype(jnp.float32).reshape(2, row_total, groups, group_cols)
    real_part, imag_part = across_groups(values[0], values[1], groups, -1.0)
    column_index = lax.broadcasted_iota(jnp.int32, (1, 1, group_cols), 2)
    group_index = lax.broadcasted_iota(jnp.int32, (1, groups, 1), 1)
    real_part, imag_part = twiddle(
        real_part, imag_part, column_index, group_index, -1.0, total_length
    )
    real_part, imag_part = long_transform(real_part, imag_part, -1.0)
    real_part = real_part * obliquity[None]
    imag_part = imag_part * obliquity[None]
    real_part, imag_part = long_transform(real_part, imag_part, 1.0)
    real_part, imag_part = twiddle(
        real_part, imag_part, column_index, group_index, 1.0, total_length
    )
    real_part, imag_part = across_groups(real_part, imag_part, groups, 1.0)
    inverse_scale = 1.0 / total_length
    returned = jnp.stack([real_part * inverse_scale, imag_part * inverse_scale])
    return returned.reshape(2, row_total, total_length).astype(jnp.bfloat16)


def through_rows(panel_rows, obliquity):
    moved_rows = lax.all_to_all(panel_rows, "rcv", split_axis=1, concat_axis=2, tiled=True)
    returned = filter_rows(moved_rows, obliquity, lax.axis_size("rcv"))
    return lax.all_to_all(returned, "rcv", split_axis=2, concat_axis=1, tiled=True)


def complex_product(left_rows, right_rows):
    left_joined = jnp.concatenate([left_rows[0], left_rows[1]], axis=0)
    upper = jnp.concatenate([right_rows[0], right_rows[1]], axis=1)
    lower = jnp.concatenate([-right_rows[1], right_rows[0]], axis=1)
    right_joined = jnp.concatenate([upper, lower], axis=0)
    return lax.dot_general(
        left_joined, right_joined, (((0,), (0,)), ((), ())), preferred_element_type=jnp.float32
    )


def per_device(recorded, obliquity, clip_level):
    spacing = N // K
    row_total = recorded.shape[1]
    col_total = recorded.shape[2]
    panel_rows = recorded.reshape(2, row_total // spacing, spacing, col_total)[:, :, 0, :]
    filtered = through_rows(panel_rows, obliquity)
    clip_rows = clip_level[:, None]
    estimate = recorded
    passes = []
    for update_index in range(2):
        columns = estimate.reshape(2, row_total, col_total // spacing, spacing)[:, :, :, 0]
        left_local = jnp.swapaxes(columns, 1, 2)
        left_panel = lax.all_gather(left_local, "rcv", axis=1, tiled=True)

        def accumulate(running, panel_piece, first_row, left_all=left_panel):
            return complex_product(left_all, panel_piece)

        zeros_init = jnp.zeros((row_total, 2 * col_total), jnp.float32)
        product_sum = accumulate(
            zeros_init, lax.all_gather(filtered, "src", axis=1, tiled=True), jnp.int32(0)
        )
        pred_real = product_sum[:, :col_total]
        pred_imag = product_sum[:, col_total:]
        limiter = lax.rsqrt(
            1.0 + (pred_real * pred_real + pred_imag * pred_imag) / (clip_rows * clip_rows)
        )
        estimate = (
            recorded.astype(jnp.float32) - jnp.stack([pred_real * limiter, pred_imag * limiter])
        ).astype(jnp.bfloat16)
        passes.append(estimate)
    return (passes[0], passes[1])


def solution(mesh):
    return jax.shard_map(
        per_device,
        mesh=mesh,
        in_specs=(P(None, "src", "rcv"), P(), P("src")),
        out_specs=(P(None, "src", "rcv"), P(None, "src", "rcv")),
        check_vma=False,
    )
```

profile of v0, /device:TPU:0, one launch (start us, length us, event | category | flops | bytes accessed | tf_op | source)
XLA Modules:
  0.0 1766.5 jit_solution(15114326470105082469)
XLA Ops:
  7.2 3.3 slice.86
  10.5 1.7 copy.102
  12.1 6.3 all-to-all-start
  18.4 41.7 %copy.64 = bf16[2,2048,4096]{1,2,0:T(8,128)(2,1)} copy(bf16[2,2048,4096]{2,1,0:T(8,128)(2,1)} %param.3) | data formatting | bytes 67108864 | tf_op args[0]
  60.2 3.0 slice.83
  63.2 1.1 copy.100
  64.3 264.5 %broadcast_multiply_fusion = (f32[4096,4096]{1,0:T(8,128)}, f32[4096,4096]{1,0:T(8,128)}) fusion(), kind=kLoop, calls=%fused_computation.33 | loop fusion | flops 251658240 | bytes 134217728 | tf_op jit(solution)/shard_map/mul | solution.py:31
  328.9 244.8 %fusion.23 = f32[4096,4096]{1,0:T(8,128)} fusion(), kind=kLoop, calls=%fused_computation.37 | loop fusion | flops 268435456 | bytes 67108864 | tf_op jit(solution)/shard_map/neg | solution.py:33
  573.7 247.6 %fusion.20 = (f32[4096,4096]{1,0:T(8,128)}, f32[4096,4096]{1,0:T(8,128)}) fusion(), kind=kLoop, calls=%fused_computation.34 | loop fusion | flops 251658240 | bytes 134217728 | tf_op jit(solution)/shard_map/sin | solution.py:31
  821.3 1.1 fusion.53
  822.4 0.5 broadcast_multiply_fusion.1
  823.0 0.4 copy.101
  823.4 0.6 fusion.48
  824.0 0.6 fusion.49
  824.6 0.6 convolution_add_fusion.1
  825.3 0.9 subtract_bitcast_fusion
  826.2 0.3 pad_maximum_fusion.6
  826.5 249.3 %fusion.2 = f32[8,4,8192]{2,0,1:T(8,128)S(1)} fusion(f32[4096,4096]{1,0:T(8,128)} %get-tuple-element.21, f32[4096,4096]{1,0:T(8,128)} %fusion.23, f32[4096,4096]{1,0:T(8,128)} %get-tuple-element.20, f32[8,4,8192]{2,1,0:T(4,128)S(1)} %pad_maximum_fusion.6), kind=kOutput, calls=%fused_computation.6 | convolution fusion | flops 25971130368 | bytes 203423744 | tf_op jit(solution)/shard_map/dot_general | solution.py:40
  1075.7 0.1 slice_multiply_fusion.1
  1075.9 235.1 %fusion.6 = f32[8,4,8192]{2,0,1:T(8,128)S(1)} fusion(f32[4096,4096]{1,0:T(8,128)} %get-tuple-element.21, f32[4096,4096]{1,0:T(8,128)} %get-tuple-element.23, f32[4096,4096]{1,0:T(8,128)} %get-tuple-element.22, f32[8,4,4096]{2,0,1:T(8,128)S(1)} %get-tuple-element.17, f32[8,4,4096]{2,0,1:T(8,128)S(1)} %get-tuple-element.16), kind=kOutput, calls=%fused_computation.9 | convolution fusion | flops 25971392512 | bytes 203423744 | tf_op jit(solution)/shard_map/dot_general | solution.py:40
  1311.0 0.1 multiply_add_fusion
  1311.2 1.2 fusion.46
  1312.4 1.3 fusion.28
  1313.7 0.2 stack.27
  1313.9 1.2 fusion.44
  1315.1 1.3 fusion.29
  1316.4 0.2 stack.28
  1316.7 12.6 copy.73
  1329.3 10.7 reshape.103
  1340.0 18.8 %all_to_all.33 = bf16[4,2,32768]{2,1,0:T(2,128)(2,1)S(1)} all-to-all(bf16[4,2,32768]{2,1,0:T(2,128)(2,1)S(1)} %reshape.103), channel_id=1, replica_groups=mesh['src'=8,'rcv'=4] {'rcv'}, dimensions={0} | all-to-all | bytes 1048576 | tf_op jit(solution)/shard_map/all_to_all | solution.py:93
  1358.8 11.0 reshape.104
  1369.8 18.9 %copy.80 = bf16[2,8,4,4096]{3,2,1,0:T(4,128)(2,1)S(1)} copy(bf16[2,8,4,4096]{1,0,3,2:T(2,128)(2,1)} %bitcast.103) | data formatting | bytes 1048576 | tf_op jit(solution)/shard_map/all_to_all | solution.py:93
  1388.7 1.1 copy.103
  1389.9 2.7 slice_bitcast_fusion.5
  1392.6 33.2 %all-gather.6.cloned.1.call-done = bf16[2,256,4096]{2,1,0:T(8,128)(2,1)} async-done(((bf16[2,32,4096]{2,1,0:T(8,128)(2,1)}), bf16[2,256,4096]{2,1,0:T(8,128)(2,1)}) %all-gather.6.cloned.1.call-update) | async-done | bytes 4194320 | tf_op jit(solution)/shard_map/all_gather | solution.py:125
  1425.8 4.7 slice_bitcast_fusion
  1430.5 1.7 fusion.118
  1432.2 30.1 %fusion.31 = f32[2048,8192]{1,0:T(8,128)} fusion(bf16[256,4096]{1,0:T(8,128)(2,1)} %get-tuple-element.7, bf16[256,4096]{1,0:T(8,128)(2,1)S(1)} %fusion.118, bf16[256,4096]{1,0:T(8,128)(2,1)} %get-tuple-element.6, bf16[256,2048]{1,0:T(8,128)(2,1)} %get-tuple-element.11, bf16[256,2048]{1,0:T(8,128)(2,1)S(1)} %get-tuple-element.10), kind=kOutput, calls=%fused_computation.50 | convolution fusion | flops 17217617920 | bytes 75497472 | tf_op jit(solution)/shard_map/dot_general | solution.py:101
  1462.4 43.9 %multiply_bitcast_fusion.3 = (f32[1,2048,4096]{2,1,0:T(8,128)}, f32[1,2048,4096]{2,1,0:T(8,128)}) fusion(f32[2048,8192]{1,0:T(8,128)} %fusion.31, f32[2048]{0:T(1024)S(1)} %mul.357), kind=kLoop, calls=%fused_computation.31 | loop fusion | flops 58720256 | bytes 134225920 | tf_op jit(solution)/shard_map/stack | solution.py:133
  1506.3 42.3 %fusion.12 = bf16[2,2048,4096]{2,1,0:T(8,128)(2,1)} fusion(bf16[2,2048,4096]{2,1,0:T(8,128)(2,1)} %param.3, f32[1,2048,4096]{2,1,0:T(8,128)} %get-tuple-element.5, f32[1,2048,4096]{2,1,0:T(8,128)} %get-tuple-element.4), kind=kLoop, calls=%fused_computation.19 | loop fusion | flops 67108864 | bytes 134217728 | tf_op jit(solution)/shard_map/convert_element_type | solution.py:134
  1548.6 41.7 %copy.76 = bf16[2,2048,4096]{1,2,0:T(8,128)(2,1)} copy(bf16[2,2048,4096]{2,1,0:T(8,128)(2,1)} %fusion.12) | data formatting | bytes 67108864 | tf_op jit(solution)/shard_map/convert_element_type | solution.py:134
  1590.3 3.0 slice.97
  1593.3 1.1 copy.99
  1594.5 46.1 %all-gather.8.cloned.1.call-done = bf16[2,256,2048]{2,1,0:T(8,128)(2,1)} async-done(((bf16[2,64,2048]{2,1,0:T(8,128)(2,1)}), bf16[2,256,2048]{2,1,0:T(8,128)(2,1)}) %all-gather.8.cloned.1.call-update) | async-done | bytes 2097168 | tf_op jit(solution)/shard_map/all_gather | solution.py:118
  1640.6 2.7 slice_bitcast_fusion.3
  1643.3 30.1 %fusion.30 = f32[2048,8192]{1,0:T(8,128)} fusion(bf16[256,4096]{1,0:T(8,128)(2,1)} %get-tuple-element.7, bf16[256,4096]{1,0:T(8,128)(2,1)S(1)} %fusion.118, bf16[256,4096]{1,0:T(8,128)(2,1)} %get-tuple-element.6, bf16[256,2048]{1,0:T(8,128)(2,1)} %get-tuple-element.9, bf16[256,2048]{1,0:T(8,128)(2,1)S(1)} %get-tuple-element.8), kind=kOutput, calls=%fused_computation.49 | convolution fusion | flops 17217617920 | bytes 75497472 | tf_op jit(solution)/shard_map/dot_general | solution.py:101
  1673.4 43.8 %multiply_bitcast_fusion.1 = (f32[1,2048,4096]{2,1,0:T(8,128)}, f32[1,2048,4096]{2,1,0:T(8,128)}) fusion(f32[2048,8192]{1,0:T(8,128)} %fusion.30, f32[2048]{0:T(1024)S(1)} %mul.357), kind=kLoop, calls=%fused_computation.28 | loop fusion | flops 58720256 | bytes 134225920 | tf_op jit(solution)/shard_map/stack | solution.py:133
  1717.2 42.3 %fusion.13 = bf16[2,2048,4096]{2,1,0:T(8,128)(2,1)} fusion(bf16[2,2048,4096]{2,1,0:T(8,128)(2,1)} %param.3, f32[1,2048,4096]{2,1,0:T(8,128)} %get-tuple-element.3, f32[1,2048,4096]{2,1,0:T(8,128)} %get-tuple-element.2), kind=kLoop, calls=%fused_computation.20 | loop fusion | flops 67108864 | bytes 134217728 | tf_op jit(solution)/shard_map/convert_element_type | solution.py:134
  (20 shorter events, 0.2 us)
Async XLA Ops:
  12.1 810.9 %all-to-all-start = ((bf16[2,32,4096]{2,0,1:T(2,128)(2,1)}), bf16[2,32,4096]{2,0,1:T(2,128)(2,1)S(1)}, u32[]{:S(2)}, u32[]{:S(2)}) async-start(bf16[2,32,4096]{2,0,1:T(2,128)(2,1)} %bitcast.97), calls=%async_computation | async-start | bytes 1048576 | tf_op jit(solution)/shard_map/all_to_all | solution.py:91
  18.4 1371.5 %all-gather.4.cloned.1.call-start = ((), (), s32[]{:S(2)}) async-start(), calls=%async_computation.2 | async-start | bytes 2621440 | tf_op jit(solution)/shard_map/all_gather | solution.py:118
  64.3 1361.5 %all-gather.6.cloned.1.call-start = ((), (), s32[]{:S(2)}) async-start(), calls=%async_computation.3 | async-start | bytes 4718592 | tf_op jit(solution)/shard_map/all_gather | solution.py:125
  823.0 3.2 copy-start
  826.5 249.3 %copy-start.3 = (f32[4,4096]{1,0:T(4,128)S(1)}, f32[4,4096]{1,0:T(4,128)}, u32[]{:S(2)}) copy-start(f32[4,4096]{1,0:T(4,128)} %param.4) | copy-start | bytes 196612
  1075.8 235.2 %copy-start.1 = (f32[4,4096]{1,0:T(4,128)S(1)}, f32[4,4096]{1,0:T(4,128)}, u32[]{:S(2)}) copy-start(f32[4,4096]{1,0:T(4,128)} %copy-done) | copy-start | bytes 196612
  1075.9 235.2 %copy-start.2 = (f32[4,4096]{1,0:T(4,128)S(1)}, f32[4,4096]{1,0:T(4,128)}, u32[]{:S(2)}) copy-start(f32[4,4096]{1,0:T(4,128)} %fusion.53) | copy-start | bytes 196612
  1311.0 78.9 %copy-start.4 = (f32[2048]{0:T(1024)S(1)}, f32[2048]{0:T(1024)}, u32[]{:S(2)}) copy-start(f32[2048]{0:T(1024)} %param.5) | copy-start | bytes 24580
  1389.8 250.7 %all-gather.8.cloned.1.call-start = ((), (), s32[]{:S(2)}) async-start(), calls=%async_computation.4 | async-start | bytes 2621440 | tf_op jit(solution)/shard_map/all_gather | solution.py:118
Sparse Core Ops, SparseCore 0:
  64.4 47.4 all-gather.3
  1390.0 35.8 all-gather.5
  1594.6 45.9 all-gather.7
where the time goes:
time: 1780 us; the launch traced here: 1770 us
  other arithmetic  933 us (52%)
  matrix products  552 us (31%)
  local copies, waits for them, and re-layouts  162 us (9%)
  waiting for transfers between devices  79.4 us (4%)
  blocking collectives  18.8 us (1%)
    dot_general x2, matrix products, long_transform(): jnp.dot(joined.reshape(-1, 2 * length), long_table(length, orient), preci...  484 us
    mul x1, other arithmetic, long_table(): sine_part = orient * jnp.sin(angles)  265 us
    sin x1, other arithmetic, long_table(): sine_part = orient * jnp.sin(angles)  248 us
    neg x1, other arithmetic, long_table(): lower = jnp.concatenate([-sine_part, cosine], axis=1)  245 us
    another operation x2, other arithmetic, per_device(): jnp.stack([pred_real * limiter, pred_imag * limiter])  87.7 us
    convert_element_type x2, other arithmetic, per_device(): estimate = (recorded.astype(jnp.float32) - jnp.stack([pred_real * limiter...  84.7 us
    unnamed x15, local copies, waits for them, and re-layouts  65.6 us
    dot_general x2, matrix products, complex_product(): lax.dot_general(left_joined, right_joined, (((0,), (0,)), ((), ())), pref...  60.3 us
  transfers between devices with their start and end apart: 4, of which 2 were waited for; matrix products, arithmetic and copies ran while one was open for 77% of the time, Pallas kernels for 0%

commit v1 on v0

--- a/solution.py
+++ b/solution.py
@@ -1,18 +1,237 @@
+import functools
 import math
 
 import jax
 import jax.numpy as jnp
+import numpy as np
 from jax import lax
+from jax.experimental import pallas as pl
+from jax.experimental.pallas import tpu as pltpu
 from jax.sharding import PartitionSpec as P
 
-N = 16384
-K = 256
+LANES = 128
+PANEL = 256
+BF16 = jnp.bfloat16
+F32 = jnp.float32
+VMEM_BYTES = 56 * 2**20
+
+
+class Sizes:
+    def __init__(self, recorded, n_src, n_rcv):
+        self.n_src, self.n_rcv = n_src, n_rcv
+        self.rows, self.cols = recorded.shape[1], recorded.shape[2]
+        self.order = self.cols * n_rcv
+        self.spacing = self.order // PANEL
+        self.group = PANEL // n_src
+        self.own = self.group // n_rcv
+        self.panel_cols = PANEL // n_rcv
+        self.slots = self.cols // LANES
+        self.points = self.order // LANES
+        self.halves = LANES // self.spacing
+        self.depth = 2 * PANEL
+
+    def fits(self):
+        return (
+            self.points == LANES
+            and self.n_src & (self.n_src - 1) == 0
+            and self.n_src > 2
+            and self.group % self.n_rcv == 0
+            and self.own % 8 == 0
+            and self.panel_cols % self.group == 0
+            and 2 * self.panel_cols == LANES
+            and self.spacing % 16 == 0
+            and self.halves * LANES == PANEL
+            and self.rows % 256 == 0
+        )
+
+
+def transform_tables(points, order):
+    index = np.arange(points)
+    angles = np.outer(index, index) % points * (2.0 * math.pi / points)
+    cosine, sine = np.cos(angles), np.sin(angles)
+    table = np.block([[cosine, sine], [-sine, cosine]]).astype(np.float32)
+    high = table.astype(BF16)
+    low = (table - high.astype(np.float32)).astype(BF16)
+    turns = np.outer(index, np.arange(LANES)) % order * (2.0 * math.pi / order)
+    factors = np.stack([np.cos(turns), np.sin(turns)]).astype(np.float32)
+    return np.stack([high, low, high.T, low.T]), factors
+
+
+def lane_parts(lane, s):
+    group, rest = lane // (2 * s.group), lane % (2 * s.group)
+    owner, rest = rest // (2 * s.own), rest % (2 * s.own)
+    part, row = rest // s.own, rest % s.own
+    return group * s.group + owner * s.own + row, part
+
+
+def pick_rows_kernel(s, recorded, *refs):
+    outs, (held, lines, sems) = refs[: s.n_rcv], refs[s.n_rcv :]
+    me = lax.axis_index("rcv")
+
+    def copy(index):
+        ahead, row = index // s.own, index % s.own
+        line = lax.rem(me + ahead, s.n_rcv) * s.own + row
+        first = pl.multiple_of(line * s.spacing, 16)
+        return pltpu.make_async_copy(
+            recorded.at[:, pl.ds(first, 16), :], held.at[index], sems.at[index]
+        )
+
+    for index in range(s.group):
+        copy(index).start()
+    for index in range(s.group):
+        copy(index).wait()
+        for part in range(2):
+            line = held[index, part].astype(F32)[0:1]
+            for slot in range(s.slots):
+                lines[slot : slot + 1, :] = line[:, slot * LANES : (slot + 1) * LANES]
+            outs[index // s.own][index % s.own, part] = lines[...].astype(BF16)
+
+
+def pick_rows(recorded, s):
+    shape = (s.own, 2, s.slots, LANES)
+    return pl.pallas_call(
+        functools.partial(pick_rows_kernel, s),
+        in_specs=[pl.BlockSpec(memory_space=pl.ANY)],
+        out_shape=[jax.ShapeDtypeStruct(shape, BF16)] * s.n_rcv,
+        scratch_shapes=[
+            pltpu.VMEM((s.group, 2, 16, s.cols), BF16),
+            pltpu.VMEM((s.slots, LANES), F32),
+            pltpu.SemaphoreType.DMA((s.group,)),
+        ],
+        compiler_params=pltpu.CompilerParams(vmem_limit_bytes=VMEM_BYTES),
+        name="pick_rows",
+    )(recorded)
+
+
+def pick_columns_kernel(s, recorded, out, select):
+    @pl.when(pl.program_id(0) == 0)
+    def _():
+        shape = (s.cols, LANES)
+        receiver = lax.broadcasted_iota(jnp.int32, shape, 0)
+        column, part = lane_parts(lax.broadcasted_iota(jnp.int32, shape, 1), s)
+        for which in range(2):
+            chosen = (receiver == column * s.spacing) & (part == which)
+            select[which] = jnp.where(chosen, 1.0, 0.0).astype(BF16)
+
+    real = jnp.dot(recorded[0], select[0], preferred_element_type=F32)
+    imag = jnp.dot(recorded[1], select[1], preferred_element_type=F32)
+    out[...] = (real + imag).astype(BF16)
+
+
+def pick_columns(recorded, s):
+    block = 256
+    return pl.pallas_call(
+        functools.partial(pick_columns_kernel, s),
+        grid=(s.rows // block,),
+        in_specs=[pl.BlockSpec((2, block, s.cols), lambda i: (0, i, 0))],
+        out_specs=pl.BlockSpec((block, LANES), lambda i: (i, 0)),
+        out_shape=jax.ShapeDtypeStruct((s.rows, LANES), BF16),
+        scratch_shapes=[pltpu.VMEM((2, s.cols, LANES), BF16)],
+        compiler_params=pltpu.CompilerParams(vmem_limit_bytes=VMEM_BYTES),
+        name="pick_columns",
+    )(recorded)
+
+
+def split(values):
+    high = values.astype(BF16)
+    return high, (values - high.astype(F32)).astype(BF16)
+
+
+def dot(left, right):
+    return jnp.dot(left, right, preferred_element_type=F32)
+
+
+def filter_kernel(s, *refs):
+    blocks, refs = refs[: s.n_rcv], refs[s.n_rcv :]
+    tables, factors, weights = refs[:3]
+    outs = refs[3 : 3 + s.n_rcv]
+    values, joined, turned, sorted_rows = refs[3 + s.n_rcv :]
+    me = lax.axis_index("rcv")
+    n = s.points
+    lanes = [slice(r * LANES, (r + 1) * LANES) for r in range(s.own)]
+    rows = [slice(r * n, (r + 1) * n) for r in range(s.own)]
+    for behind in range(s.n_rcv):
+        owner = lax.rem(me + s.n_rcv - behind, s.n_rcv)
+        for part in range(2):
+            place = pl.ds(pl.multiple_of(part * n + owner * s.slots, 16), s.slots)
+            for r in range(s.own):
+                values[place, lanes[r]] = blocks[behind][r, part]
+    cosine, sine = factors[0], factors[1]
+    first = dot(tables[0], values[...]) + dot(tables[1], values[...])
+    for r in range(s.own):
+        real, imag = first[:n, lanes[r]], first[n:, lanes[r]]
+        joined[rows[r], :LANES] = real * cosine + imag * sine
+        joined[rows[r], LANES:] = imag * cosine - real * sine
+    high, low = split(joined[...])
+    spectrum = dot(high, tables[2]) + (dot(high, tables[3]) + dot(low, tables[2]))
+    scale = jnp.concatenate([weights[...], weights[...]], axis=1)
+    for r in range(s.own):
+        joined[rows[r], :] = spectrum[rows[r]] * scale
+    high, low = split(joined[...])
+    back = dot(high, tables[0]) + (dot(high, tables[1]) + dot(low, tables[0]))
+    cosine, sine = cosine * (1.0 / s.order), sine * (1.0 / s.order)
+    for r in range(s.own):
+        real, imag = back[rows[r], :LANES], back[rows[r], LANES:]
+        turned[:n, lanes[r]] = real * cosine - imag * sine
+        turned[n:, lanes[r]] = real * sine + imag * cosine
+    high, low = split(turned[...])
+    result = dot(tables[2], high) + (dot(tables[3], high) + dot(tables[2], low))
+
+    shape = (s.halves * s.own, s.own * LANES)
+    wanted = lax.broadcasted_iota(jnp.int32, shape, 0)
+    lane = lax.broadcasted_iota(jnp.int32, shape, 1)
+    chosen = lane == (wanted % s.own) * LANES + (wanted // s.own) * s.spacing
+    select = jnp.where(chosen, 1.0, 0.0).astype(BF16)
+    rounded = result.astype(BF16)
+    picked = [
+        lax.dot_general(
+            select,
+            rounded[part * n : (part + 1) * n],
+            (((1,), (1,)), ((), ())),
+            preferred_element_type=F32,
+        )
+        for part in range(2)
+    ]
+    for half in range(s.halves):
+        place = slice(half * s.own, (half + 1) * s.own)
+        extra = jnp.concatenate([picked[0][place], picked[1][place]], axis=0).astype(BF16)
+        for out in outs:
+            out[s.slots + half] = extra
+
+    height = 2 * s.own
+    for part in range(2):
+        for r in range(s.own):
+            place = pl.ds(part * s.own + r, n, stride=height)
+            sorted_rows[place, :] = result[part * n : (part + 1) * n, lanes[r]]
+    for ahead in range(s.n_rcv):
+        owner = lax.rem(me + ahead, s.n_rcv)
+        first_row = pl.multiple_of(owner * s.slots * height, 16)
+        mine = sorted_rows[pl.ds(first_row, s.slots * height), :]
+        outs[ahead][: s.slots] = mine.reshape(s.slots, height, LANES).astype(BF16)
+
+
+def filter_rows(blocks, obliquity, s):
+    tables, factors = transform_tables(s.points, s.order)
+    weights = jnp.transpose(jnp.transpose(obliquity).reshape(LANES, s.points))
+    shape = (s.slots + s.halves, 2 * s.own, LANES)
+    return pl.pallas_call(
+        functools.partial(filter_kernel, s),
+        out_shape=[jax.ShapeDtypeStruct(shape, BF16)] * s.n_rcv,
+        scratch_shapes=[
+            pltpu.VMEM((2 * s.points, s.own * LANES), BF16),
+            pltpu.VMEM((s.own * s.points, 2 * LANES), F32),
+            pltpu.VMEM((2 * s.points, s.own * LANES), F32),
+            pltpu.VMEM((2 * s.own * s.points, LANES), F32),
+        ],
+        compiler_params=pltpu.CompilerParams(vmem_limit_bytes=VMEM_BYTES),
+        name="filter_rows",
+    )(*blocks, jnp.asarray(tables), jnp.asarray(factors), weights)
 
 
 TWO_PI = 2.0 * math.pi
 
 
-def rotate(real_part, imag_part, cosine, sine_part):
+def turn(real_part, imag_part, cosine, sine_part):
     return (real_part * cosine - imag_part * sine_part, real_part * sine_part + imag_part * cosine)
 
 
@@ -20,7 +239,7 @@
     angles = (column_index * group_index % total_length).astype(jnp.float32) * (
         TWO_PI / total_length
     )
-    return rotate(real_part, imag_part, jnp.cos(angles), orient * jnp.sin(angles))
+    return turn(real_part, imag_part, jnp.cos(angles), orient * jnp.sin(angles))
 
 
 def long_table(length, orient):
@@ -63,7 +282,7 @@
     return (new_real, new_imag)
 
 
-def filter_rows(whole_rows, obliquity, groups):
+def plain_filter(whole_rows, obliquity, groups):
     row_total = whole_rows.shape[1]
     group_cols = whole_rows.shape[2] // groups
     total_length = groups * group_cols
@@ -89,7 +308,7 @@
 
 def through_rows(panel_rows, obliquity):
     moved_rows = lax.all_to_all(panel_rows, "rcv", split_axis=1, concat_axis=2, tiled=True)
-    returned = filter_rows(moved_rows, obliquity, lax.axis_size("rcv"))
+    returned = plain_filter(moved_rows, obliquity, lax.axis_size("rcv"))
     return lax.all_to_all(returned, "rcv", split_axis=2, concat_axis=1, tiled=True)
 
 
@@ -103,8 +322,8 @@
     )
 
 
-def per_device(recorded, obliquity, clip_level):
-    spacing = N // K
+def plain_device(recorded, obliquity, clip_level):
+    spacing = recorded.shape[2] * lax.axis_size("rcv") // PANEL
     row_total = recorded.shape[1]
     col_total = recorded.shape[2]
     panel_rows = recorded.reshape(2, row_total // spacing, spacing, col_total)[:, :, 0, :]
@@ -136,6 +355,172 @@
     return (passes[0], passes[1])
 
 
+def limited(real, imag, clip, clip_squared):
+    return clip * lax.rsqrt(clip_squared + (real * real + imag * imag))
+
+
+def update_kernel(s, tile_rows, tile_slots, *refs):
+    count = 2 * s.n_rcv - 1
+    recorded, clip_rows = refs[:2]
+    left_blocks, refs = refs[2 : 2 + count], refs[2 + count :]
+    filtered, refs = refs[: s.n_src * s.n_rcv], refs[s.n_src * s.n_rcv :]
+    out_first, out_second, right, own_columns, left, sems = refs
+    src, rcv = lax.axis_index("src"), lax.axis_index("rcv")
+    width = tile_slots * LANES
+
+    @pl.when(pl.program_id(0) == 0)
+    def _():
+        copies = []
+        for across in range(s.n_src):
+            for behind in range(s.n_rcv):
+                index = across * s.n_rcv + behind
+                owner = lax.rem(rcv + s.n_rcv - behind, s.n_rcv)
+                place = (src ^ across) * s.n_rcv + owner
+                copies.append(
+                    pltpu.make_async_copy(filtered[index], right.at[place], sems.at[index])
+                )
+        for copy in copies:
+            copy.start()
+        for copy in copies:
+            copy.wait()
+        row = lax.broadcasted_iota(jnp.int32, (PANEL, s.depth), 0)
+        lane = lax.broadcasted_iota(jnp.int32, (PANEL, s.depth), 1)
+        column, _part = lane_parts(lane % LANES, s)
+        column = column + (lane // LANES) * s.panel_cols
+        chosen = row == (column % s.halves) * LANES + column // s.halves
+        spread = jnp.where(chosen, 1.0, 0.0).astype(BF16)
+        held = [right[:, s.slots + h].reshape(s.depth, LANES) for h in range(s.halves)]
+        own_columns[...] = dot(jnp.concatenate(held, axis=1), spread).astype(BF16)
+
+    clip = clip_rows[...]
+    clip_squared = clip * clip
+
+    own, before, after = left_blocks[0], left_blocks[1 : s.n_rcv], left_blocks[s.n_rcv :]
+    blocks = []
+    for place in range(s.n_rcv):
+        block = own[...]
+        for at in range(s.n_rcv):
+            if at > place:
+                block = jnp.where(rcv == at, before[at - place - 1][...], block)
+            elif at < place:
+                block = jnp.where(rcv == at, after[place - at - 1][...], block)
+        blocks.append(block.astype(F32))
+    plain = jnp.concatenate(blocks, axis=1)
+    lane = lax.broadcasted_iota(jnp.int32, (tile_rows, s.depth), 1)
+    is_real = (lane // s.own) % 2 == 0
+    swapped = jnp.where(
+        is_real,
+        pltpu.roll(plain, s.depth - s.own, 1),
+        pltpu.roll(plain, s.own, 1),
+    )
+    sign = jnp.where(is_real, 1.0, -1.0)
+    signed = plain * sign
+    left[:tile_rows] = signed.astype(BF16)
+    left[tile_rows : 2 * tile_rows] = swapped.astype(BF16)
+
+    product = dot(left[: 2 * tile_rows], own_columns[...])
+    real, imag = product[:tile_rows], product[tile_rows:]
+    limiter = limited(real, imag, clip, clip_squared)
+    real, imag = real * limiter, imag * limiter
+    left[2 * tile_rows : 3 * tile_rows] = (signed - jnp.where(is_real, real, -imag)).astype(BF16)
+    left[3 * tile_rows :] = (swapped - jnp.where(is_real, imag, real)).astype(BF16)
+
+    for tile in range(s.slots // tile_slots):
+        place = slice(tile * width, (tile + 1) * width)
+        slots = range(tile * tile_slots, (tile + 1) * tile_slots)
+        pieces = [right[:, slot].reshape(s.depth, LANES) for slot in slots]
+        product = dot(left[...], jnp.concatenate(pieces, axis=1))
+        base_real = recorded[0, :, place].astype(F32)
+        base_imag = recorded[1, :, place].astype(F32)
+        for which, out in enumerate((out_first, out_second)):
+            first = 2 * which * tile_rows
+            real = product[first : first + tile_rows]
+            imag = product[first + tile_rows : first + 2 * tile_rows]
+            limiter = limited(real, imag, clip, clip_squared)
+            out[0, :, place] = (base_real - real * limiter).astype(BF16)
+            out[1, :, place] = (base_imag - imag * limiter).astype(BF16)
+
+
+def update(recorded, clip_level, left_blocks, filtered, s):
+    tile_rows, tile_slots = 128, 2
+    block = pl.BlockSpec((2, tile_rows, s.cols), lambda i: (0, i, 0))
+    left_block = pl.BlockSpec((tile_rows, LANES), lambda i: (i, 0))
+    places = s.n_src * s.n_rcv
+    product_flops = 16 * s.rows * s.cols * PANEL
+    return pl.pallas_call(
+        functools.partial(update_kernel, s, tile_rows, tile_slots),
+        grid=(s.rows // tile_rows,),
+        in_specs=[block, pl.BlockSpec((tile_rows, 1), lambda i: (i, 0))]
+        + [left_block] * len(left_blocks)
+        + [pl.BlockSpec(memory_space=pl.ANY)] * places,
+        out_specs=[block, block],
+        out_shape=[jax.ShapeDtypeStruct(recorded.shape, BF16)] * 2,
+        scratch_shapes=[
+            pltpu.VMEM((places, s.slots + s.halves, 2 * s.own, LANES), BF16),
+            pltpu.VMEM((s.depth, s.depth), BF16),
+            pltpu.VMEM((4 * tile_rows, s.depth), BF16),
+            pltpu.SemaphoreType.DMA((places,)),
+        ],
+        compiler_params=pltpu.CompilerParams(vmem_limit_bytes=VMEM_BYTES),
+        cost_estimate=pl.CostEstimate(
+            flops=product_flops, bytes_accessed=6 * 2 * s.rows * s.cols, transcendentals=0
+        ),
+        name="update",
+    )(recorded, clip_level[:, None], *left_blocks, *filtered)
+
+
+def rotate(block, ahead, count):
+    pairs = [(at, (at + ahead) % count) for at in range(count)]
+    return lax.ppermute(block, "rcv", pairs)
+
+
+def exchange(blocks, count):
+    return [blocks[0]] + [rotate(blocks[k], k, count) for k in range(1, count)]
+
+
+def gather_line(block, count):
+    up = [(at, at + 1) for at in range(count - 1)]
+    down = [(at + 1, at) for at in range(count - 1)]
+    before, after = [], []
+    up_block = down_block = block
+    for _ in range(count - 1):
+        up_block = lax.ppermute(up_block, "rcv", up)
+        down_block = lax.ppermute(down_block, "rcv", down)
+        before.append(up_block)
+        after.append(down_block)
+    return [block] + before + after
+
+
+def gather_cube(pieces, count):
+    steps = [1 << bit for bit in range(1, count.bit_length() - 1)]
+    half = len(pieces) // 2
+    gathered = {}
+    for order, part in ((steps, range(half)), (steps[::-1], range(half, len(pieces)))):
+        for which in part:
+            held = {0: pieces[which]}
+            for step in order:
+                pairs = [(at, at ^ step) for at in range(count)]
+                held.update(
+                    {d ^ step: lax.ppermute(p, "src", pairs) for d, p in sorted(held.items())}
+                )
+            pairs = [(at, at ^ 1) for at in range(count)]
+            held.update({d ^ 1: lax.ppermute(p, "src", pairs) for d, p in sorted(held.items())})
+            for d, p in held.items():
+                gathered[d, which] = p
+    return [gathered[d, which] for d in range(count) for which in range(len(pieces))]
+
+
+def per_device(recorded, obliquity, clip_level):
+    s = Sizes(recorded, lax.axis_size("src"), lax.axis_size("rcv"))
+    if not s.fits():
+        return plain_device(recorded, obliquity, clip_level)
+    moved = exchange(pick_rows(recorded, s), s.n_rcv)
+    left_blocks = gather_line(pick_columns(recorded, s), s.n_rcv)
+    returned = exchange(filter_rows(moved, obliquity, s), s.n_rcv)
+    filtered = gather_cube(returned, s.n_src)
+    return update(recorded, clip_level, left_blocks, filtered, s)
+
+
 def solution(mesh):
     return jax.shard_map(
         per_device,

time: 1780 us -> 172 us (0.10)
  other arithmetic: 933 us -> 0 us
  matrix products: 552 us -> 0 us
  local copies, waits for them, and re-layouts: 162 us -> 6.48 us
  Pallas kernels: 0 us -> 84.2 us
  waiting for transfers between devices: 79.4 us -> 29.4 us
  starting transfers between devices: 6.4 us -> 49.8 us
  blocking collectives: 18.8 us -> 0 us
    dot_general x12 -> x0, matrix products: 552 us -> none  [the longest x2 484 us: long_transform(): jnp.dot(joined.reshape(-1, 2 * length), long_table(length, orient), preci...]
    mul x4 -> x0, other arithmetic: 265 us -> none  [the longest x1 265 us: long_table(): sine_part = orient * jnp.sin(angles)]
    sin x2 -> x0, other arithmetic: 249 us -> none  [the longest x1 248 us: long_table(): sine_part = orient * jnp.sin(angles)]
    neg x2 -> x0, other arithmetic: 247 us -> none  [the longest x1 245 us: long_table(): lower = jnp.concatenate([-sine_part, cosine], axis=1)]
    another operation x3 -> x0, other arithmetic: 87.7 us -> none  [the longest x2 87.7 us: per_device(): jnp.stack([pred_real * limiter, pred_imag * limiter])]
    convert_element_type x2 -> x0, other arithmetic: 84.7 us -> none  [per_device(): estimate = (recorded.astype(jnp.float32) - jnp.stack([pred_real * limiter...]
    pallas_call x0 -> x4, Pallas kernels: none -> 84.2 us  [the longest x1 57.9 us: update(): pl.pallas_call(functools.partial(update_kernel, s, tile_rows, tile_slots)...]
    all_gather x3 -> x0, waiting for transfers between devices: 79.3 us -> none  [the longest x2 46.1 us: per_device(): left_panel = lax.all_gather(left_local, 'rcv', axis=1, tiled=True)]
  transfers between devices with their start and end apart: 4 -> 40, of which waited for: 2 -> 15; matrix products, arithmetic and copies ran while one was open for 77% -> 3% of each run, Pallas kernels for 0% -> 13%
where the time goes in v1:
time: 172 us; the launch traced here: 171 us
  Pallas kernels  84.2 us (49%)
  starting transfers between devices  49.8 us (29%)
  waiting for transfers between devices  29.4 us (17%)
  local copies, waits for them, and re-layouts  6.48 us (4%)
    pallas_call x1, Pallas kernels, update(): pl.pallas_call(functools.partial(update_kernel, s, tile_rows, tile_slots)...  57.9 us
    ppermute x28, waiting for transfers between devices, gather_cube(): lax.ppermute(p, 'src', pairs)  21.1 us
    ppermute x3, starting transfers between devices, gather_line(): up_block = lax.ppermute(up_block, 'rcv', up)  19.5 us
    pallas_call x1, Pallas kernels, pick_columns(): pl.pallas_call(functools.partial(pick_columns_kernel, s), grid=(s.rows //...  16.9 us
    ppermute x28, starting transfers between devices, gather_cube(): lax.ppermute(p, 'src', pairs)  15.6 us
    ppermute x6, starting transfers between devices, rotate(): return lax.ppermute(block, 'rcv', pairs)  10.8 us
    ppermute x6, waiting for transfers between devices, rotate(): return lax.ppermute(block, 'rcv', pairs)  6.87 us
    pallas_call x1, Pallas kernels, filter_rows(): pl.pallas_call(functools.partial(filter_kernel, s), out_shape=[jax.ShapeD...  4.97 us
  transfers between devices with their start and end apart: 40, of which 15 were waited for; matrix products, arithmetic and copies ran while one was open for 3% of the time, Pallas kernels for 13%

profile of v1, /device:TPU:0, one launch (start us, length us, event | category | flops | bytes accessed | tf_op | source)
XLA Modules:
  0.0 171.0 jit_solution(17407375240142249253)
XLA Ops:
  0.6 4.4 %pick_rows.1 = (bf16[8,2,32,128]{3,2,1,0:T(8,128)(2,1)}, bf16[8,2,32,128]{3,2,1,0:T(8,128)(2,1)}, bf16[8,2,32,128]{3,2,1,0:T(8,128)(2,1)}, bf16[8,2,32,128]{3,2,1,0:T(8,128)(2,1)}) custom-call(bf16[2,2048,4096]{2,1,0:T(8,128)(2,1)} %refs_0_.1), custom_call_target="tpu_custom_call" | custom-call | tf_op jit(solution)/shard_map/pick_rows/pallas_call | solution.py:92
  5.1 3.1 %collective-permute-start.6 = (bf16[8,2,32,128]{3,2,1,0:T(8,128)(2,1)}, bf16[8,2,32,128]{3,2,1,0:T(8,128)(2,1)S(1)}, u32[]{:S(2)}, u32[]{:S(2)}) collective-permute-start(bf16[8,2,32,128]{3,2,1,0:T(8,128)(2,1)} %get-tuple-element.11), channel_id=1, source_target_pairs={{0,1},{1,2},{2,3},{3,0},{4,5},{5,6},{6,7},{7,4},{8,9},{9,10},{10,1... | collective-permute-start | bytes 393224 | tf_op jit(solution)/shard_map/ppermute | solution.py:474
  8.2 2.6 %collective-permute-start.7 = (bf16[8,2,32,128]{3,2,1,0:T(8,128)(2,1)}, bf16[8,2,32,128]{3,2,1,0:T(8,128)(2,1)S(1)}, u32[]{:S(2)}, u32[]{:S(2)}) collective-permute-start(bf16[8,2,32,128]{3,2,1,0:T(8,128)(2,1)} %get-tuple-element.12), channel_id=1, source_target_pairs={{0,2},{1,3},{2,0},{3,1},{4,6},{5,7},{6,4},{7,5},{8,10},{9,11},{10,... | collective-permute-start | bytes 393224 | tf_op jit(solution)/shard_map/ppermute | solution.py:474
  10.8 1.3 collective-permute-start.8
  12.1 16.9 %pick_columns.1.refs_2_ = bf16[2048,128]{1,0:T(8,128)(2,1)} custom-call(bf16[2,2048,4096]{2,1,0:T(8,128)(2,1)} %refs_0_.1), custom_call_target="tpu_custom_call" | custom-call | tf_op jit(solution)/shard_map/pick_columns/pallas_call | solution.py:123
  29.0 1.3 collective-permute-start.3
  30.3 5.4 %collective-permute-start = (bf16[2048,128]{1,0:T(8,128)(2,1)}, bf16[2048,128]{1,0:T(8,128)(2,1)}, u32[]{:S(2)}, u32[]{:S(2)}) collective-permute-start(bf16[2048,128]{1,0:T(8,128)(2,1)} %pick_columns.1.refs_2_), channel_id=1, source_target_pairs={{0,1},{1,2},{2,3},{4,5},{5,6},{6,7},{8,9},{9,10},{10,11},{12,13},{... | collective-permute-start | bytes 1572872 | tf_op jit(solution)/shard_map/ppermute | solution.py:487
  35.7 0.6 copy.7
  36.3 1.6 reshape.7
  38.0 0.7 copy.8
  38.7 0.6 copy-done
  39.4 5.0 %filter_rows.1 = (bf16[34,16,128]{2,1,0:T(8,128)(2,1)}, bf16[34,16,128]{2,1,0:T(8,128)(2,1)}, bf16[34,16,128]{2,1,0:T(8,128)(2,1)}, bf16[34,16,128]{2,1,0:T(8,128)(2,1)}) custom-call(bf16[8,2,32,128]{3,2,1,0:T(8,128)(2,1)} %get-tuple-element.10.refs_0_, bf16[8,2,32,128]{3,2,1,0:T(8,128)(2,1)} %copy-done, bf16[8,2,32,128]{3,2,1,0:T(8,128)(2,1)} %copy-done.1, ...), custom_call_target="tpu_custom_call" | custom-call | tf_op jit(solution)/shard_map/filter_rows/pallas_call | solution.py:217
  44.4 3.8 %collective-permute-start.11 = (bf16[34,16,128]{2,1,0:T(8,128)(2,1)}, bf16[34,16,128]{2,1,0:T(8,128)(2,1)S(1)}, u32[]{:S(2)}, u32[]{:S(2)}) collective-permute-start(bf16[34,16,128]{2,1,0:T(8,128)(2,1)} %get-tuple-element.17), channel_id=1, source_target_pairs={{0,3},{1,0},{2,1},{3,2},{4,7},{5,4},{6,5},{7,6},{8,11},{9,8},{10,9... | collective-permute-start | bytes 417800 | tf_op jit(solution)/shard_map/ppermute | solution.py:474
  48.2 4.8 %collective-permute-done.9.refs_10_ = bf16[34,16,128]{2,1,0:T(8,128)(2,1)S(1)} collective-permute-done((bf16[34,16,128]{2,1,0:T(8,128)(2,1)}, bf16[34,16,128]{2,1,0:T(8,128)(2,1)S(1)}, u32[]{:S(2)}, u32[]{:S(2)}) %collective-permute-start.9) | collective-permute-done | bytes 139296 | tf_op jit(solution)/shard_map/ppermute | solution.py:474
  53.1 1.5 collective-permute-start.24
  54.6 2.0 %collective-permute-done.10.refs_11_ = bf16[34,16,128]{2,1,0:T(8,128)(2,1)S(1)} collective-permute-done((bf16[34,16,128]{2,1,0:T(8,128)(2,1)}, bf16[34,16,128]{2,1,0:T(8,128)(2,1)S(1)}, u32[]{:S(2)}, u32[]{:S(2)}) %collective-permute-start.10) | collective-permute-done | bytes 139296 | tf_op jit(solution)/shard_map/ppermute | solution.py:474
  56.6 1.5 collective-permute-start.16
  58.1 0.2 collective-permute-done.24.refs_25_
  58.3 1.5 collective-permute-start.25
  59.8 2.0 %collective-permute-done.16.refs_17_ = bf16[34,16,128]{2,1,0:T(8,128)(2,1)S(1)} collective-permute-done((bf16[34,16,128]{2,1,0:T(8,128)(2,1)}, bf16[34,16,128]{2,1,0:T(8,128)(2,1)S(1)}, u32[]{:S(2)}, u32[]{:S(2)}) %collective-permute-start.16) | collective-permute-done | bytes 139296 | tf_op jit(solution)/shard_map/ppermute | solution.py:504
  61.9 1.8 %collective-permute-start.17 = (bf16[34,16,128]{2,1,0:T(8,128)(2,1)S(1)}, bf16[34,16,128]{2,1,0:T(8,128)(2,1)S(1)}, u32[]{:S(2)}, u32[]{:S(2)}) collective-permute-start(bf16[34,16,128]{2,1,0:T(8,128)(2,1)S(1)} %collective-permute-done.9.refs_10_), channel_id=1, source_target_pairs={{0,8},{4,12},{8,0},{12,4},{16,24},{20,28},{24,16},{28,20},{1,9},{5... | collective-permute-start | bytes 417800 | tf_op jit(solution)/shard_map/ppermute | solution.py:504
  63.7 0.5 collective-permute-done.25.refs_26_
  64.2 2.2 %collective-permute-start.26 = (bf16[34,16,128]{2,1,0:T(8,128)(2,1)S(1)}, bf16[34,16,128]{2,1,0:T(8,128)(2,1)S(1)}, u32[]{:S(2)}, u32[]{:S(2)}) collective-permute-start(bf16[34,16,128]{2,1,0:T(8,128)(2,1)S(1)} %collective-permute-done.10.refs_11_), channel_id=1, source_target_pairs={{0,16},{4,20},{8,24},{12,28},{16,0},{20,4},{24,8},{28,12},{1,17},{... | collective-permute-start | bytes 417800 | tf_op jit(solution)/shard_map/ppermute | solution.py:504
  66.3 1.3 collective-permute-start.4
  67.6 4.6 %collective-permute-start.1 = (bf16[2048,128]{1,0:T(8,128)(2,1)}, bf16[2048,128]{1,0:T(8,128)(2,1)S(1)}, u32[]{:S(2)}, u32[]{:S(2)}) collective-permute-start(bf16[2048,128]{1,0:T(8,128)(2,1)} %collective-permute-done.refs_3_), channel_id=1, source_target_pairs={{0,1},{1,2},{2,3},{4,5},{5,6},{6,7},{8,9},{9,10},{10,11},{12,13},{... | collective-permute-start | bytes 1572872 | tf_op jit(solution)/shard_map/ppermute | solution.py:487
  72.2 1.2 collective-permute-start.18
  73.5 0.6 collective-permute-start.27
  74.1 3.4 %collective-permute-done.18.refs_19_ = bf16[34,16,128]{2,1,0:T(8,128)(2,1)S(1)} collective-permute-done((bf16[34,16,128]{2,1,0:T(8,128)(2,1)S(1)}, bf16[34,16,128]{2,1,0:T(8,128)(2,1)S(1)}, u32[]{:S(2)}, u32[]{:S(2)}) %collective-permute-start.18) | collective-permute-done | bytes 139296 | tf_op jit(solution)/shard_map/ppermute | solution.py:504
  77.5 1.0 collective-permute-start.19
  78.5 1.0 collective-permute-done.27.refs_28_
  79.6 3.0 %collective-permute-done.19.refs_20_ = bf16[34,16,128]{2,1,0:T(8,128)(2,1)S(1)} collective-permute-done((bf16[34,16,128]{2,1,0:T(8,128)(2,1)S(1)}, bf16[34,16,128]{2,1,0:T(8,128)(2,1)S(1)}, u32[]{:S(2)}, u32[]{:S(2)}) %collective-permute-start.19) | collective-permute-done | bytes 139296 | tf_op jit(solution)/shard_map/ppermute | solution.py:504
  82.6 0.3 collective-permute-start.32
  82.9 0.5 collective-permute-start.29
  83.4 5.0 %collective-permute-done.32.refs_33_ = bf16[34,16,128]{2,1,0:T(8,128)(2,1)S(1)} collective-permute-done((bf16[34,16,128]{2,1,0:T(8,128)(2,1)S(1)}, bf16[34,16,128]{2,1,0:T(8,128)(2,1)S(1)}, u32[]{:S(2)}, u32[]{:S(2)}) %collective-permute-start.32) | collective-permute-done | bytes 139296 | tf_op jit(solution)/shard_map/ppermute | solution.py:504
  88.5 1.5 collective-permute-start.34
  90.0 1.3 collective-permute-start.5
  91.3 9.5 %collective-permute-start.2 = (bf16[2048,128]{1,0:T(8,128)(2,1)S(1)}, bf16[2048,128]{1,0:T(8,128)(2,1)S(1)}, u32[]{:S(2)}, u32[]{:S(2)}) collective-permute-start(bf16[2048,128]{1,0:T(8,128)(2,1)S(1)} %collective-permute-done.1.refs_4_), channel_id=1, source_target_pairs={{0,1},{1,2},{2,3},{4,5},{5,6},{6,7},{8,9},{9,10},{10,11},{12,13},{... | collective-permute-start | bytes 1572872 | tf_op jit(solution)/shard_map/ppermute | solution.py:487
  101.0 0.5 collective-permute-start.22
  101.6 0.7 collective-permute-done.30.refs_31_
  102.5 0.4 collective-permute-start.23
  102.9 4.4 %collective-permute-done.35.refs_36_ = bf16[34,16,128]{2,1,0:T(8,128)(2,1)} collective-permute-done((bf16[34,16,128]{2,1,0:T(8,128)(2,1)S(1)}, bf16[34,16,128]{2,1,0:T(8,128)(2,1)}, u32[]{:S(2)}, u32[]{:S(2)}) %collective-permute-start.35) | collective-permute-done | bytes 139296 | tf_op jit(solution)/shard_map/ppermute | solution.py:504
  107.3 0.6 collective-permute-start.37
  108.0 0.7 collective-permute-done.36.refs_37_
  108.8 0.5 copy-done.34
  109.3 1.4 copy.9.refs_1_
  110.9 1.2 collective-permute-done.2.refs_5_
  112.2 0.8 copy-done.9
  113.0 57.9 %update.1 = (bf16[2,2048,4096]{2,1,0:T(8,128)(2,1)}, bf16[2,2048,4096]{2,1,0:T(8,128)(2,1)}) custom-call(bf16[2,2048,4096]{2,1,0:T(8,128)(2,1)} %refs_0_.1, f32[2048,1]{1,0:T(8,128)} %copy.9.refs_1_, bf16[2048,128]{1,0:T(8,128)(2,1)} %pick_columns.1.refs_2_, bf16[2048,128]{1,0:T(8,128)(2,1)} %collective-permute-done.refs_3_, bf16[2048,128]{1,0:T(8,128)(2,1)} %copy-done.7, ...), custom_call_target="tpu_custom_call" | custom-call | flops 34359738368 | bytes 100663296 | tf_op jit(solution)/shard_map/update/pallas_call | solution.py:450
  (110 shorter events, 1.2 us)
Async XLA Ops:
  0.6 108.7 %copy-start.4 = (f32[2048]{0:T(1024)S(1)}, f32[2048]{0:T(1024)}, u32[]{:S(2)}) copy-start(f32[2048]{0:T(1024)} %param.7) | copy-start | bytes 24580
  5.1 33.6 %collective-permute-start.6 = (bf16[8,2,32,128]{3,2,1,0:T(8,128)(2,1)}, bf16[8,2,32,128]{3,2,1,0:T(8,128)(2,1)S(1)}, u32[]{:S(2)}, u32[]{:S(2)}) collective-permute-start(bf16[8,2,32,128]{3,2,1,0:T(8,128)(2,1)} %get-tuple-element.11), channel_id=1, source_target_pairs={{0,1},{1,2},{2,3},{3,0},{4,5},{5,6},{6,7},{7,4},{8,9},{9,10},{10,1... | collective-permute-start | bytes 393224 | tf_op jit(solution)/shard_map/ppermute | solution.py:474
  8.2 30.5 %collective-permute-start.7 = (bf16[8,2,32,128]{3,2,1,0:T(8,128)(2,1)}, bf16[8,2,32,128]{3,2,1,0:T(8,128)(2,1)S(1)}, u32[]{:S(2)}, u32[]{:S(2)}) collective-permute-start(bf16[8,2,32,128]{3,2,1,0:T(8,128)(2,1)} %get-tuple-element.12), channel_id=1, source_target_pairs={{0,2},{1,3},{2,0},{3,1},{4,6},{5,7},{6,4},{7,5},{8,10},{9,11},{10,... | collective-permute-start | bytes 393224 | tf_op jit(solution)/shard_map/ppermute | solution.py:474
  10.8 27.9 %collective-permute-start.8 = (bf16[8,2,32,128]{3,2,1,0:T(8,128)(2,1)}, bf16[8,2,32,128]{3,2,1,0:T(8,128)(2,1)S(1)}, u32[]{:S(2)}, u32[]{:S(2)}) collective-permute-start(bf16[8,2,32,128]{3,2,1,0:T(8,128)(2,1)} %get-tuple-element.13), channel_id=1, source_target_pairs={{0,3},{1,0},{2,1},{3,2},{4,7},{5,4},{6,5},{7,6},{8,11},{9,8},{10,9... | collective-permute-start | bytes 393224 | tf_op jit(solution)/shard_map/ppermute | solution.py:474
  29.0 37.3 %collective-permute-start.3 = (bf16[2048,128]{1,0:T(8,128)(2,1)}, bf16[2048,128]{1,0:T(8,128)(2,1)S(1)}, u32[]{:S(2)}, u32[]{:S(2)}) collective-permute-start(bf16[2048,128]{1,0:T(8,128)(2,1)} %pick_columns.1.refs_2_), channel_id=1, source_target_pairs={{1,0},{2,1},{3,2},{5,4},{6,5},{7,6},{9,8},{10,9},{11,10},{13,12},{... | collective-permute-start | bytes 1572872 | tf_op jit(solution)/shard_map/ppermute | solution.py:488
  30.3 37.3 %collective-permute-start = (bf16[2048,128]{1,0:T(8,128)(2,1)}, bf16[2048,128]{1,0:T(8,128)(2,1)}, u32[]{:S(2)}, u32[]{:S(2)}) collective-permute-start(bf16[2048,128]{1,0:T(8,128)(2,1)} %pick_columns.1.refs_2_), channel_id=1, source_target_pairs={{0,1},{1,2},{2,3},{4,5},{5,6},{6,7},{8,9},{9,10},{10,11},{12,13},{... | collective-permute-start | bytes 1572872 | tf_op jit(solution)/shard_map/ppermute | solution.py:487
  44.4 8.7 %collective-permute-start.9 = (bf16[34,16,128]{2,1,0:T(8,128)(2,1)}, bf16[34,16,128]{2,1,0:T(8,128)(2,1)S(1)}, u32[]{:S(2)}, u32[]{:S(2)}) collective-permute-start(bf16[34,16,128]{2,1,0:T(8,128)(2,1)} %get-tuple-element.15), channel_id=1, source_target_pairs={{0,1},{1,2},{2,3},{3,0},{4,5},{5,6},{6,7},{7,4},{8,9},{9,10},{10,1... | collective-permute-start | bytes 417800 | tf_op jit(solution)/shard_map/ppermute | solution.py:474
  44.4 12.2 %collective-permute-start.10 = (bf16[34,16,128]{2,1,0:T(8,128)(2,1)}, bf16[34,16,128]{2,1,0:T(8,128)(2,1)S(1)}, u32[]{:S(2)}, u32[]{:S(2)}) collective-permute-start(bf16[34,16,128]{2,1,0:T(8,128)(2,1)} %get-tuple-element.16), channel_id=1, source_target_pairs={{0,2},{1,3},{2,0},{3,1},{4,6},{5,7},{6,4},{7,5},{8,10},{9,11},{10,... | collective-permute-start | bytes 417800 | tf_op jit(solution)/shard_map/ppermute | solution.py:474
  44.4 13.7 %collective-permute-start.11 = (bf16[34,16,128]{2,1,0:T(8,128)(2,1)}, bf16[34,16,128]{2,1,0:T(8,128)(2,1)S(1)}, u32[]{:S(2)}, u32[]{:S(2)}) collective-permute-start(bf16[34,16,128]{2,1,0:T(8,128)(2,1)} %get-tuple-element.17), channel_id=1, source_target_pairs={{0,3},{1,0},{2,1},{3,2},{4,7},{5,4},{6,5},{7,6},{8,11},{9,8},{10,9... | collective-permute-start | bytes 417800 | tf_op jit(solution)/shard_map/ppermute | solution.py:474
  53.1 59.1 %copy-start.10 = (bf16[34,16,128]{2,1,0:T(8,128)(2,1)}, bf16[34,16,128]{2,1,0:T(8,128)(2,1)S(1)}, u32[]{:S(2)}) copy-start(bf16[34,16,128]{2,1,0:T(8,128)(2,1)S(1)} %collective-permute-done.9.refs_10_) | copy-start | bytes 417796
  53.1 5.3 %collective-permute-start.24 = (bf16[34,16,128]{2,1,0:T(8,128)(2,1)}, bf16[34,16,128]{2,1,0:T(8,128)(2,1)S(1)}, u32[]{:S(2)}, u32[]{:S(2)}) collective-permute-start(bf16[34,16,128]{2,1,0:T(8,128)(2,1)} %get-tuple-element.14.refs_9_), channel_id=1, source_target_pairs={{0,16},{4,20},{8,24},{12,28},{16,0},{20,4},{24,8},{28,12},{1,17},{... | collective-permute-start | bytes 417800 | tf_op jit(solution)/shard_map/ppermute | solution.py:504
  56.6 55.6 %copy-start.11 = (bf16[34,16,128]{2,1,0:T(8,128)(2,1)}, bf16[34,16,128]{2,1,0:T(8,128)(2,1)S(1)}, u32[]{:S(2)}) copy-start(bf16[34,16,128]{2,1,0:T(8,128)(2,1)S(1)} %collective-permute-done.10.refs_11_) | copy-start | bytes 417796
  56.6 5.3 %collective-permute-start.16 = (bf16[34,16,128]{2,1,0:T(8,128)(2,1)}, bf16[34,16,128]{2,1,0:T(8,128)(2,1)S(1)}, u32[]{:S(2)}, u32[]{:S(2)}) collective-permute-start(bf16[34,16,128]{2,1,0:T(8,128)(2,1)} %get-tuple-element.14.refs_9_), channel_id=1, source_target_pairs={{0,8},{4,12},{8,0},{12,4},{16,24},{20,28},{24,16},{28,20},{1,9},{5... | collective-permute-start | bytes 417800 | tf_op jit(solution)/shard_map/ppermute | solution.py:504
  58.1 54.1 %copy-start.12 = (bf16[34,16,128]{2,1,0:T(8,128)(2,1)}, bf16[34,16,128]{2,1,0:T(8,128)(2,1)S(1)}, u32[]{:S(2)}) copy-start(bf16[34,16,128]{2,1,0:T(8,128)(2,1)S(1)} %collective-permute-done.11.refs_12_) | copy-start | bytes 417796
  58.1 5.6 %collective-permute-start.12 = (bf16[34,16,128]{2,1,0:T(8,128)(2,1)}, bf16[34,16,128]{2,1,0:T(8,128)(2,1)S(1)}, u32[]{:S(2)}, u32[]{:S(2)}) collective-permute-start(bf16[34,16,128]{2,1,0:T(8,128)(2,1)} %get-tuple-element.14.refs_9_), channel_id=1, source_target_pairs={{0,4},{4,0},{8,12},{12,8},{16,20},{20,16},{24,28},{28,24},{1,5},{5... | collective-permute-start | bytes 417800 | tf_op jit(solution)/shard_map/ppermute | solution.py:507
  58.3 53.8 %copy-start.13 = (bf16[34,16,128]{2,1,0:T(8,128)(2,1)}, bf16[34,16,128]{2,1,0:T(8,128)(2,1)S(1)}, u32[]{:S(2)}) copy-start(bf16[34,16,128]{2,1,0:T(8,128)(2,1)S(1)} %collective-permute-done.24.refs_25_) | copy-start | bytes 417796
  58.3 5.8 %collective-permute-start.25 = (bf16[34,16,128]{2,1,0:T(8,128)(2,1)S(1)}, bf16[34,16,128]{2,1,0:T(8,128)(2,1)S(1)}, u32[]{:S(2)}, u32[]{:S(2)}) collective-permute-start(bf16[34,16,128]{2,1,0:T(8,128)(2,1)S(1)} %collective-permute-done.9.refs_10_), channel_id=1, source_target_pairs={{0,16},{4,20},{8,24},{12,28},{16,0},{20,4},{24,8},{28,12},{1,17},{... | collective-permute-start | bytes 417800 | tf_op jit(solution)/shard_map/ppermute | solution.py:504
  61.9 50.3 %copy-start.14 = (bf16[34,16,128]{2,1,0:T(8,128)(2,1)}, bf16[34,16,128]{2,1,0:T(8,128)(2,1)S(1)}, u32[]{:S(2)}) copy-start(bf16[34,16,128]{2,1,0:T(8,128)(2,1)S(1)} %collective-permute-done.16.refs_17_) | copy-start | bytes 417796
  61.9 10.4 %collective-permute-start.17 = (bf16[34,16,128]{2,1,0:T(8,128)(2,1)S(1)}, bf16[34,16,128]{2,1,0:T(8,128)(2,1)S(1)}, u32[]{:S(2)}, u32[]{:S(2)}) collective-permute-start(bf16[34,16,128]{2,1,0:T(8,128)(2,1)S(1)} %collective-permute-done.9.refs_10_), channel_id=1, source_target_pairs={{0,8},{4,12},{8,0},{12,4},{16,24},{20,28},{24,16},{28,20},{1,9},{5... | collective-permute-start | bytes 417800 | tf_op jit(solution)/shard_map/ppermute | solution.py:504
  63.7 48.5 %copy-start.15 = (bf16[34,16,128]{2,1,0:T(8,128)(2,1)}, bf16[34,16,128]{2,1,0:T(8,128)(2,1)S(1)}, u32[]{:S(2)}) copy-start(bf16[34,16,128]{2,1,0:T(8,128)(2,1)S(1)} %collective-permute-done.12.refs_13_) | copy-start | bytes 417796
  63.7 9.8 %collective-permute-start.13 = (bf16[34,16,128]{2,1,0:T(8,128)(2,1)S(1)}, bf16[34,16,128]{2,1,0:T(8,128)(2,1)S(1)}, u32[]{:S(2)}, u32[]{:S(2)}) collective-permute-start(bf16[34,16,128]{2,1,0:T(8,128)(2,1)S(1)} %collective-permute-done.9.refs_10_), channel_id=1, source_target_pairs={{0,4},{4,0},{8,12},{12,8},{16,20},{20,16},{24,28},{28,24},{1,5},{5... | collective-permute-start | bytes 417800 | tf_op jit(solution)/shard_map/ppermute | solution.py:507
  64.2 9.3 %collective-permute-start.26 = (bf16[34,16,128]{2,1,0:T(8,128)(2,1)S(1)}, bf16[34,16,128]{2,1,0:T(8,128)(2,1)S(1)}, u32[]{:S(2)}, u32[]{:S(2)}) collective-permute-start(bf16[34,16,128]{2,1,0:T(8,128)(2,1)S(1)} %collective-permute-done.10.refs_11_), channel_id=1, source_target_pairs={{0,16},{4,20},{8,24},{12,28},{16,0},{20,4},{24,8},{28,12},{1,17},{... | collective-permute-start | bytes 417800 | tf_op jit(solution)/shard_map/ppermute | solution.py:504
  66.3 45.8 %copy-start.5 = (bf16[2048,128]{1,0:T(8,128)(2,1)}, bf16[2048,128]{1,0:T(8,128)(2,1)S(1)}, u32[]{:S(2)}) copy-start(bf16[2048,128]{1,0:T(8,128)(2,1)S(1)} %collective-permute-done.3.refs_6_) | copy-start | bytes 1572868
  66.3 23.6 %collective-permute-start.4 = (bf16[2048,128]{1,0:T(8,128)(2,1)S(1)}, bf16[2048,128]{1,0:T(8,128)(2,1)S(1)}, u32[]{:S(2)}, u32[]{:S(2)}) collective-permute-start(bf16[2048,128]{1,0:T(8,128)(2,1)S(1)} %collective-permute-done.3.refs_6_), channel_id=1, source_target_pairs={{1,0},{2,1},{3,2},{5,4},{6,5},{7,6},{9,8},{10,9},{11,10},{13,12},{... | collective-permute-start | bytes 1572872 | tf_op jit(solution)/shard_map/ppermute | solution.py:488
  67.6 23.7 %collective-permute-start.1 = (bf16[2048,128]{1,0:T(8,128)(2,1)}, bf16[2048,128]{1,0:T(8,128)(2,1)S(1)}, u32[]{:S(2)}, u32[]{:S(2)}) collective-permute-start(bf16[2048,128]{1,0:T(8,128)(2,1)} %collective-permute-done.refs_3_), channel_id=1, source_target_pairs={{0,1},{1,2},{2,3},{4,5},{5,6},{6,7},{8,9},{9,10},{10,11},{12,13},{... | collective-permute-start | bytes 1572872 | tf_op jit(solution)/shard_map/ppermute | solution.py:487
  72.2 5.2 %collective-permute-start.18 = (bf16[34,16,128]{2,1,0:T(8,128)(2,1)S(1)}, bf16[34,16,128]{2,1,0:T(8,128)(2,1)S(1)}, u32[]{:S(2)}, u32[]{:S(2)}) collective-permute-start(bf16[34,16,128]{2,1,0:T(8,128)(2,1)S(1)} %collective-permute-done.10.refs_11_), channel_id=1, source_target_pairs={{0,8},{4,12},{8,0},{12,4},{16,24},{20,28},{24,16},{28,20},{1,9},{5... | collective-permute-start | bytes 417800 | tf_op jit(solution)/shard_map/ppermute | solution.py:504
  73.5 5.1 %collective-permute-start.14 = (bf16[34,16,128]{2,1,0:T(8,128)(2,1)S(1)}, bf16[34,16,128]{2,1,0:T(8,128)(2,1)S(1)}, u32[]{:S(2)}, u32[]{:S(2)}) collective-permute-start(bf16[34,16,128]{2,1,0:T(8,128)(2,1)S(1)} %collective-permute-done.10.refs_11_), channel_id=1, source_target_pairs={{0,4},{4,0},{8,12},{12,8},{16,20},{20,16},{24,28},{28,24},{1,5},{5... | collective-permute-start | bytes 417800 | tf_op jit(solution)/shard_map/ppermute | solution.py:507
  73.5 6.1 %collective-permute-start.27 = (bf16[34,16,128]{2,1,0:T(8,128)(2,1)S(1)}, bf16[34,16,128]{2,1,0:T(8,128)(2,1)S(1)}, u32[]{:S(2)}, u32[]{:S(2)}) collective-permute-start(bf16[34,16,128]{2,1,0:T(8,128)(2,1)S(1)} %collective-permute-done.11.refs_12_), channel_id=1, source_target_pairs={{0,16},{4,20},{8,24},{12,28},{16,0},{20,4},{24,8},{28,12},{1,17},{... | collective-permute-start | bytes 417800 | tf_op jit(solution)/shard_map/ppermute | solution.py:504
  77.5 5.1 %collective-permute-start.19 = (bf16[34,16,128]{2,1,0:T(8,128)(2,1)S(1)}, bf16[34,16,128]{2,1,0:T(8,128)(2,1)S(1)}, u32[]{:S(2)}, u32[]{:S(2)}) collective-permute-start(bf16[34,16,128]{2,1,0:T(8,128)(2,1)S(1)} %collective-permute-done.11.refs_12_), channel_id=1, source_target_pairs={{0,8},{4,12},{8,0},{12,4},{16,24},{20,28},{24,16},{28,20},{1,9},{5... | collective-permute-start | bytes 417800 | tf_op jit(solution)/shard_map/ppermute | solution.py:504
  78.5 4.4 %collective-permute-start.15 = (bf16[34,16,128]{2,1,0:T(8,128)(2,1)S(1)}, bf16[34,16,128]{2,1,0:T(8,128)(2,1)S(1)}, u32[]{:S(2)}, u32[]{:S(2)}) collective-permute-start(bf16[34,16,128]{2,1,0:T(8,128)(2,1)S(1)} %collective-permute-done.11.refs_12_), channel_id=1, source_target_pairs={{0,4},{4,0},{8,12},{12,8},{16,20},{20,16},{24,28},{28,24},{1,5},{5... | collective-permute-start | bytes 417800 | tf_op jit(solution)/shard_map/ppermute | solution.py:507
  79.6 3.3 %collective-permute-start.28 = (bf16[34,16,128]{2,1,0:T(8,128)(2,1)S(1)}, bf16[34,16,128]{2,1,0:T(8,128)(2,1)S(1)}, u32[]{:S(2)}, u32[]{:S(2)}) collective-permute-start(bf16[34,16,128]{2,1,0:T(8,128)(2,1)S(1)} %collective-permute-done.24.refs_25_), channel_id=1, source_target_pairs={{0,4},{4,0},{8,12},{12,8},{16,20},{20,16},{24,28},{28,24},{1,5},{5... | collective-permute-start | bytes 417800 | tf_op jit(solution)/shard_map/ppermute | solution.py:507
  82.6 5.8 %collective-permute-start.32 = (bf16[34,16,128]{2,1,0:T(8,128)(2,1)S(1)}, bf16[34,16,128]{2,1,0:T(8,128)(2,1)S(1)}, u32[]{:S(2)}, u32[]{:S(2)}) collective-permute-start(bf16[34,16,128]{2,1,0:T(8,128)(2,1)S(1)} %collective-permute-done.16.refs_17_), channel_id=1, source_target_pairs={{0,16},{4,20},{8,24},{12,28},{16,0},{20,4},{24,8},{28,12},{1,17},{... | collective-permute-start | bytes 417800 | tf_op jit(solution)/shard_map/ppermute | solution.py:504
  82.9 5.5 %collective-permute-start.20 = (bf16[34,16,128]{2,1,0:T(8,128)(2,1)S(1)}, bf16[34,16,128]{2,1,0:T(8,128)(2,1)S(1)}, u32[]{:S(2)}, u32[]{:S(2)}) collective-permute-start(bf16[34,16,128]{2,1,0:T(8,128)(2,1)S(1)} %collective-permute-done.16.refs_17_), channel_id=1, source_target_pairs={{0,4},{4,0},{8,12},{12,8},{16,20},{20,16},{24,28},{28,24},{1,5},{5... | collective-permute-start | bytes 417800 | tf_op jit(solution)/shard_map/ppermute | solution.py:507
  82.9 5.6 %collective-permute-start.29 = (bf16[34,16,128]{2,1,0:T(8,128)(2,1)S(1)}, bf16[34,16,128]{2,1,0:T(8,128)(2,1)S(1)}, u32[]{:S(2)}, u32[]{:S(2)}) collective-permute-start(bf16[34,16,128]{2,1,0:T(8,128)(2,1)S(1)} %collective-permute-done.25.refs_26_), channel_id=1, source_target_pairs={{0,4},{4,0},{8,12},{12,8},{16,20},{20,16},{24,28},{28,24},{1,5},{5... | collective-permute-start | bytes 417800 | tf_op jit(solution)/shard_map/ppermute | solution.py:507
  88.4 12.5 %collective-permute-start.33 = (bf16[34,16,128]{2,1,0:T(8,128)(2,1)S(1)}, bf16[34,16,128]{2,1,0:T(8,128)(2,1)}, u32[]{:S(2)}, u32[]{:S(2)}) collective-permute-start(bf16[34,16,128]{2,1,0:T(8,128)(2,1)S(1)} %collective-permute-done.17.refs_18_), channel_id=1, source_target_pairs={{0,16},{4,20},{8,24},{12,28},{16,0},{20,4},{24,8},{28,12},{1,17},{... | collective-permute-start | bytes 417800 | tf_op jit(solution)/shard_map/ppermute | solution.py:504
  88.4 12.6 %collective-permute-start.21 = (bf16[34,16,128]{2,1,0:T(8,128)(2,1)S(1)}, bf16[34,16,128]{2,1,0:T(8,128)(2,1)S(1)}, u32[]{:S(2)}, u32[]{:S(2)}) collective-permute-start(bf16[34,16,128]{2,1,0:T(8,128)(2,1)S(1)} %collective-permute-done.17.refs_18_), channel_id=1, source_target_pairs={{0,4},{4,0},{8,12},{12,8},{16,20},{20,16},{24,28},{28,24},{1,5},{5... | collective-permute-start | bytes 417800 | tf_op jit(solution)/shard_map/ppermute | solution.py:507
  88.5 13.0 %collective-permute-start.34 = (bf16[34,16,128]{2,1,0:T(8,128)(2,1)S(1)}, bf16[34,16,128]{2,1,0:T(8,128)(2,1)}, u32[]{:S(2)}, u32[]{:S(2)}) collective-permute-start(bf16[34,16,128]{2,1,0:T(8,128)(2,1)S(1)} %collective-permute-done.26.refs_27_), channel_id=1, source_target_pairs={{0,8},{4,12},{8,0},{12,4},{16,24},{20,28},{24,16},{28,20},{1,9},{5... | collective-permute-start | bytes 417800 | tf_op jit(solution)/shard_map/ppermute | solution.py:504
  90.0 20.9 %collective-permute-start.5 = (bf16[2048,128]{1,0:T(8,128)(2,1)S(1)}, bf16[2048,128]{1,0:T(8,128)(2,1)S(1)}, u32[]{:S(2)}, u32[]{:S(2)}) collective-permute-start(bf16[2048,128]{1,0:T(8,128)(2,1)S(1)} %collective-permute-done.4.refs_7_), channel_id=1, source_target_pairs={{1,0},{2,1},{3,2},{5,4},{6,5},{7,6},{9,8},{10,9},{11,10},{13,12},{... | collective-permute-start | bytes 1572872 | tf_op jit(solution)/shard_map/ppermute | solution.py:488
  91.3 20.8 %collective-permute-start.2 = (bf16[2048,128]{1,0:T(8,128)(2,1)S(1)}, bf16[2048,128]{1,0:T(8,128)(2,1)S(1)}, u32[]{:S(2)}, u32[]{:S(2)}) collective-permute-start(bf16[2048,128]{1,0:T(8,128)(2,1)S(1)} %collective-permute-done.1.refs_4_), channel_id=1, source_target_pairs={{0,1},{1,2},{2,3},{4,5},{5,6},{6,7},{8,9},{9,10},{10,11},{12,13},{... | collective-permute-start | bytes 1572872 | tf_op jit(solution)/shard_map/ppermute | solution.py:487
  100.9 1.4 collective-permute-start.30
  101.0 1.5 collective-permute-start.22
  101.5 5.8 %collective-permute-start.35 = (bf16[34,16,128]{2,1,0:T(8,128)(2,1)S(1)}, bf16[34,16,128]{2,1,0:T(8,128)(2,1)}, u32[]{:S(2)}, u32[]{:S(2)}) collective-permute-start(bf16[34,16,128]{2,1,0:T(8,128)(2,1)S(1)} %collective-permute-done.27.refs_28_), channel_id=1, source_target_pairs={{0,8},{4,12},{8,0},{12,4},{16,24},{20,28},{24,16},{28,20},{1,9},{5... | collective-permute-start | bytes 417800 | tf_op jit(solution)/shard_map/ppermute | solution.py:504
  102.3 5.0 %collective-permute-start.31 = (bf16[34,16,128]{2,1,0:T(8,128)(2,1)S(1)}, bf16[34,16,128]{2,1,0:T(8,128)(2,1)S(1)}, u32[]{:S(2)}, u32[]{:S(2)}) collective-permute-start(bf16[34,16,128]{2,1,0:T(8,128)(2,1)S(1)} %collective-permute-done.27.refs_28_), channel_id=1, source_target_pairs={{0,4},{4,0},{8,12},{12,8},{16,20},{20,16},{24,28},{28,24},{1,5},{5... | collective-permute-start | bytes 417800 | tf_op jit(solution)/shard_map/ppermute | solution.py:507
  102.5 5.4 %collective-permute-start.23 = (bf16[34,16,128]{2,1,0:T(8,128)(2,1)S(1)}, bf16[34,16,128]{2,1,0:T(8,128)(2,1)S(1)}, u32[]{:S(2)}, u32[]{:S(2)}) collective-permute-start(bf16[34,16,128]{2,1,0:T(8,128)(2,1)S(1)} %collective-permute-done.19.refs_20_), channel_id=1, source_target_pairs={{0,4},{4,0},{8,12},{12,8},{16,20},{20,16},{24,28},{28,24},{1,5},{5... | collective-permute-start | bytes 417800 | tf_op jit(solution)/shard_map/ppermute | solution.py:507
  107.3 1.4 collective-permute-start.36
  107.3 3.4 %collective-permute-start.37 = (bf16[34,16,128]{2,1,0:T(8,128)(2,1)}, bf16[34,16,128]{2,1,0:T(8,128)(2,1)}, u32[]{:S(2)}, u32[]{:S(2)}) collective-permute-start(bf16[34,16,128]{2,1,0:T(8,128)(2,1)} %collective-permute-done.33.refs_34_), channel_id=1, source_target_pairs={{0,4},{4,0},{8,12},{12,8},{16,20},{20,16},{24,28},{28,24},{1,5},{5... | collective-permute-start | bytes 417800 | tf_op jit(solution)/shard_map/ppermute | solution.py:507
  107.9 2.8 %collective-permute-start.38 = (bf16[34,16,128]{2,1,0:T(8,128)(2,1)}, bf16[34,16,128]{2,1,0:T(8,128)(2,1)}, u32[]{:S(2)}, u32[]{:S(2)}) collective-permute-start(bf16[34,16,128]{2,1,0:T(8,128)(2,1)} %collective-permute-done.34.refs_35_), channel_id=1, source_target_pairs={{0,4},{4,0},{8,12},{12,8},{16,20},{20,16},{24,28},{28,24},{1,5},{5... | collective-permute-start | bytes 417800 | tf_op jit(solution)/shard_map/ppermute | solution.py:507
  108.7 2.0 %collective-permute-start.39 = (bf16[34,16,128]{2,1,0:T(8,128)(2,1)}, bf16[34,16,128]{2,1,0:T(8,128)(2,1)}, u32[]{:S(2)}, u32[]{:S(2)}) collective-permute-start(bf16[34,16,128]{2,1,0:T(8,128)(2,1)} %collective-permute-done.35.refs_36_), channel_id=1, source_target_pairs={{0,4},{4,0},{8,12},{12,8},{16,20},{20,16},{24,28},{28,24},{1,5},{5... | collective-permute-start | bytes 417800 | tf_op jit(solution)/shard_map/ppermute | solution.py:507
  (27 other events, 319.4 us)

commit v2 on v1

--- a/solution.py
+++ b/solution.py
@@ -11,6 +11,10 @@
 
 LANES = 128
 PANEL = 256
+PIECES = 1
+ROW_BLOCK = 256
+PICK_ROWS = 512
+EARLY = 1
 BF16 = jnp.bfloat16
 F32 = jnp.float32
 VMEM_BYTES = 56 * 2**20
@@ -30,29 +34,38 @@
         self.halves = LANES // self.spacing
         self.depth = 2 * PANEL
 
+    def spans(self, extra=0):
+        count = self.slots // PIECES
+        return [(q * count, count + (extra if q == 0 else 0)) for q in range(PIECES)]
+
     def fits(self):
         return (
             self.points == LANES
             and self.n_src & (self.n_src - 1) == 0
             and self.n_src > 2
+            and self.n_rcv % 2 == 0
             and self.group % self.n_rcv == 0
             and self.own % 8 == 0
             and self.panel_cols % self.group == 0
             and 2 * self.panel_cols == LANES
             and self.spacing % 16 == 0
+            and self.slots % 16 == 0
             and self.halves * LANES == PANEL
-            and self.rows % 256 == 0
+            and self.rows % PICK_ROWS == 0
+            and self.rows > PICK_ROWS
+            and self.slots % (2 * PIECES) == 0
         )
 
 
-def transform_tables(points, order):
+def transform_tables(points, order, groups):
     index = np.arange(points)
-    angles = np.outer(index, index) % points * (2.0 * math.pi / points)
+    sorted_index = index.reshape(-1, groups).T.reshape(-1)
+    angles = np.outer(sorted_index, index) % points * (2.0 * math.pi / points)
     cosine, sine = np.cos(angles), np.sin(angles)
     table = np.block([[cosine, sine], [-sine, cosine]]).astype(np.float32)
     high = table.astype(BF16)
     low = (table - high.astype(np.float32)).astype(BF16)
-    turns = np.outer(index, np.arange(LANES)) % order * (2.0 * math.pi / order)
+    turns = np.outer(sorted_index, np.arange(LANES)) % order * (2.0 * math.pi / order)
     factors = np.stack([np.cos(turns), np.sin(turns)]).astype(np.float32)
     return np.stack([high, low, high.T, low.T]), factors
 
@@ -103,33 +116,52 @@
     )(recorded)
 
 
-def pick_columns_kernel(s, recorded, out, select):
-    @pl.when(pl.program_id(0) == 0)
+def pick_columns_kernel(s, chunk, recorded, *refs):
+    out, select, total = refs[-3:]
+    step = pl.program_id(0)
+    receiver = step * chunk + lax.broadcasted_iota(jnp.int32, (chunk, LANES), 0)
+    column, part = lane_parts(lax.broadcasted_iota(jnp.int32, (1, LANES), 1), s)
+    for which in range(2):
+        chosen = receiver == jnp.where(part == which, column * s.spacing, -1)
+        select[which] = jnp.where(chosen, 1.0, 0.0).astype(BF16)
+    picked = dot(recorded[0], select[0]) + dot(recorded[1], select[1])
+
+    @pl.when(step == 0)
     def _():
-        shape = (s.cols, LANES)
-        receiver = lax.broadcasted_iota(jnp.int32, shape, 0)
-        column, part = lane_parts(lax.broadcasted_iota(jnp.int32, shape, 1), s)
-        for which in range(2):
-            chosen = (receiver == column * s.spacing) & (part == which)
-            select[which] = jnp.where(chosen, 1.0, 0.0).astype(BF16)
-
-    real = jnp.dot(recorded[0], select[0], preferred_element_type=F32)
-    imag = jnp.dot(recorded[1], select[1], preferred_element_type=F32)
-    out[...] = (real + imag).astype(BF16)
-
-
-def pick_columns(recorded, s):
-    block = 256
+        total[...] = picked
+
+    @pl.when(step > 0)
+    def _():
+        total[...] += picked
+
+    @pl.when(step == pl.num_programs(0) - 1)
+    def _():
+        out[...] = total[...].astype(BF16)
+
+
+def pick_columns(recorded, first, count, chunk, behind, s):
+    rows = count * PICK_ROWS
     return pl.pallas_call(
-        functools.partial(pick_columns_kernel, s),
-        grid=(s.rows // block,),
-        in_specs=[pl.BlockSpec((2, block, s.cols), lambda i: (0, i, 0))],
-        out_specs=pl.BlockSpec((block, LANES), lambda i: (i, 0)),
-        out_shape=jax.ShapeDtypeStruct((s.rows, LANES), BF16),
-        scratch_shapes=[pltpu.VMEM((2, s.cols, LANES), BF16)],
+        functools.partial(pick_columns_kernel, s, chunk),
+        grid=(s.cols // chunk,),
+        in_specs=[
+            pl.BlockSpec(
+                (pl.Element(2), pl.Element(rows), pl.Element(chunk)),
+                lambda i: (0, first * PICK_ROWS, i * chunk),
+            ),
+            pl.BlockSpec(memory_space=pl.ANY),
+        ],
+        out_specs=pl.BlockSpec((rows, LANES), lambda i: (0, 0)),
+        out_shape=jax.ShapeDtypeStruct((rows, LANES), BF16),
+        scratch_shapes=[pltpu.VMEM((2, chunk, LANES), BF16), pltpu.VMEM((rows, LANES), F32)],
         compiler_params=pltpu.CompilerParams(vmem_limit_bytes=VMEM_BYTES),
+        cost_estimate=pl.CostEstimate(
+            flops=8 * rows * s.cols * LANES,
+            bytes_accessed=4 * rows * s.cols,
+            transcendentals=0,
+        ),
         name="pick_columns",
-    )(recorded)
+    )(recorded, behind)
 
 
 def split(values):
@@ -143,9 +175,11 @@
 
 def filter_kernel(s, *refs):
     blocks, refs = refs[: s.n_rcv], refs[s.n_rcv :]
-    tables, factors, weights = refs[:3]
-    outs = refs[3 : 3 + s.n_rcv]
-    values, joined, turned, sorted_rows = refs[3 + s.n_rcv :]
+    tables, factors, obliquity = refs[:3]
+    refs = refs[1:]
+    spans = s.spans()
+    outs = [refs[3 + q * s.n_rcv : 3 + (q + 1) * s.n_rcv] for q in range(len(spans))]
+    values, joined, turned, sorted_rows, factor_rows, scale = refs[3 + len(spans) * s.n_rcv :]
     me = lax.axis_index("rcv")
     n = s.points
     lanes = [slice(r * LANES, (r + 1) * LANES) for r in range(s.own)]
@@ -156,6 +190,19 @@
             place = pl.ds(pl.multiple_of(part * n + owner * s.slots, 16), s.slots)
             for r in range(s.own):
                 values[place, lanes[r]] = blocks[behind][r, part]
+
+    groups, m = obliquity.shape[0], s.points // obliquity.shape[0]
+    for a in range(groups):
+        for tile in range(m):
+            line = slice(a * m + tile, a * m + tile + 1)
+            factor_rows[line, :] = obliquity[a : a + 1, tile * LANES : (tile + 1) * LANES]
+    turned_rows = jnp.transpose(factor_rows[...])
+    for a in range(groups):
+        for q in range(groups):
+            block = turned_rows[q * m : (q + 1) * m, a * m : (a + 1) * m]
+            scale[a * m : (a + 1) * m, q * m : (q + 1) * m] = block
+            scale[a * m : (a + 1) * m, LANES + q * m : LANES + (q + 1) * m] = block
+
     cosine, sine = factors[0], factors[1]
     first = dot(tables[0], values[...]) + dot(tables[1], values[...])
     for r in range(s.own):
@@ -164,9 +211,8 @@
         joined[rows[r], LANES:] = imag * cosine - real * sine
     high, low = split(joined[...])
     spectrum = dot(high, tables[2]) + (dot(high, tables[3]) + dot(low, tables[2]))
-    scale = jnp.concatenate([weights[...], weights[...]], axis=1)
     for r in range(s.own):
-        joined[rows[r], :] = spectrum[rows[r]] * scale
+        joined[rows[r], :] = spectrum[rows[r]] * scale[...]
     high, low = split(joined[...])
     back = dot(high, tables[0]) + (dot(high, tables[1]) + dot(low, tables[0]))
     cosine, sine = cosine * (1.0 / s.order), sine * (1.0 / s.order)
@@ -195,8 +241,8 @@
     for half in range(s.halves):
         place = slice(half * s.own, (half + 1) * s.own)
         extra = jnp.concatenate([picked[0][place], picked[1][place]], axis=0).astype(BF16)
-        for out in outs:
-            out[s.slots + half] = extra
+        for out in outs[0]:
+            out[spans[0][1] + half] = extra
 
     height = 2 * s.own
     for part in range(2):
@@ -205,27 +251,32 @@
             sorted_rows[place, :] = result[part * n : (part + 1) * n, lanes[r]]
     for ahead in range(s.n_rcv):
         owner = lax.rem(me + ahead, s.n_rcv)
-        first_row = pl.multiple_of(owner * s.slots * height, 16)
-        mine = sorted_rows[pl.ds(first_row, s.slots * height), :]
-        outs[ahead][: s.slots] = mine.reshape(s.slots, height, LANES).astype(BF16)
-
-
-def filter_rows(blocks, obliquity, s):
-    tables, factors = transform_tables(s.points, s.order)
-    weights = jnp.transpose(jnp.transpose(obliquity).reshape(LANES, s.points))
-    shape = (s.slots + s.halves, 2 * s.own, LANES)
-    return pl.pallas_call(
+        for out, (start, count) in zip(outs, spans):
+            first_row = pl.multiple_of((owner * s.slots + start) * height, 16)
+            mine = sorted_rows[pl.ds(first_row, count * height), :]
+            out[ahead][:count] = mine.reshape(count, height, LANES).astype(BF16)
+
+
+def filter_rows(blocks, obliquity, behind, s):
+    tables, factors = transform_tables(s.points, s.order, obliquity.shape[0])
+    shapes = [(count, 2 * s.own, LANES) for _, count in s.spans(s.halves)]
+    outs = pl.pallas_call(
         functools.partial(filter_kernel, s),
-        out_shape=[jax.ShapeDtypeStruct(shape, BF16)] * s.n_rcv,
+        in_specs=[pl.BlockSpec(memory_space=pltpu.VMEM)] * (s.n_rcv + 3)
+        + [pl.BlockSpec(memory_space=pl.ANY)],
+        out_shape=[jax.ShapeDtypeStruct(shape, BF16) for shape in shapes for _ in range(s.n_rcv)],
         scratch_shapes=[
             pltpu.VMEM((2 * s.points, s.own * LANES), BF16),
             pltpu.VMEM((s.own * s.points, 2 * LANES), F32),
             pltpu.VMEM((2 * s.points, s.own * LANES), F32),
             pltpu.VMEM((2 * s.own * s.points, LANES), F32),
+            pltpu.VMEM((s.points, LANES), F32),
+            pltpu.VMEM((s.points, 2 * LANES), F32),
         ],
         compiler_params=pltpu.CompilerParams(vmem_limit_bytes=VMEM_BYTES),
         name="filter_rows",
-    )(*blocks, jnp.asarray(tables), jnp.asarray(factors), weights)
+    )(*blocks, jnp.asarray(tables), jnp.asarray(factors), obliquity, behind)
+    return [outs[q * s.n_rcv : (q + 1) * s.n_rcv] for q in range(len(shapes))]
 
 
 TWO_PI = 2.0 * math.pi
@@ -359,111 +410,131 @@
     return clip * lax.rsqrt(clip_squared + (real * real + imag * imag))
 
 
+def left_rows(s, left_held, rows, clip, own_columns, left):
+    rcv = lax.axis_index("rcv")
+    count = rows.size
+    blocks = []
+    for place in range(s.n_rcv):
+        block = left_held[0, rows, :]
+        for at in range(s.n_rcv):
+            if at != place:
+                source = left_held[route(at, place, s.n_rcv), rows, :]
+                block = jnp.where(rcv == at, source, block)
+        blocks.append(block.astype(F32))
+    plain = jnp.concatenate(blocks, axis=1)
+    lane = lax.broadcasted_iota(jnp.int32, (1, s.depth), 1)
+    is_real = (lane // s.own) % 2 == 0
+    swapped = jnp.where(
+        is_real,
+        pltpu.roll(plain, s.depth - s.own, 1),
+        pltpu.roll(plain, s.own, 1),
+    )
+    signed = jnp.where(is_real, plain, -plain)
+    left[:count] = signed.astype(BF16)
+    left[count : 2 * count] = swapped.astype(BF16)
+
+    product = dot(left[: 2 * count], own_columns[...])
+    real, imag = product[:count], product[count:]
+    limiter = limited(real, imag, clip, clip * clip)
+    real, imag = real * limiter, imag * limiter
+    left[2 * count : 3 * count] = (signed - jnp.where(is_real, real, -imag)).astype(BF16)
+    left[3 * count :] = (swapped - jnp.where(is_real, imag, real)).astype(BF16)
+
+
 def update_kernel(s, tile_rows, tile_slots, *refs):
-    count = 2 * s.n_rcv - 1
     recorded, clip_rows = refs[:2]
-    left_blocks, refs = refs[2 : 2 + count], refs[2 + count :]
-    filtered, refs = refs[: s.n_src * s.n_rcv], refs[s.n_src * s.n_rcv :]
-    out_first, out_second, right, own_columns, left, sems = refs
+    split_at = len(refs) - 9 - 4
+    left_blocks, filtered, refs = refs[2:split_at], refs[split_at:-9], refs[-9:]
+    out_first, out_second, right, own_columns, even, odd, sems, left_sems, left_held = refs
     src, rcv = lax.axis_index("src"), lax.axis_index("rcv")
     width = tile_slots * LANES
-
-    @pl.when(pl.program_id(0) == 0)
+    step, steps = pl.program_id(0), pl.num_programs(0)
+
+    def fill(which, left):
+        rows = pl.ds(pl.multiple_of(which * tile_rows, tile_rows), tile_rows)
+        left_rows(s, left_held, rows, clip_rows[rows, :], own_columns, left)
+
+    @pl.when(step == 0)
     def _():
         copies = []
-        for across in range(s.n_src):
+        for mask in range(s.n_src):
+            odd_mask, (half, at) = mask % 2, divmod(mask // 2, s.n_src // 4)
             for behind in range(s.n_rcv):
-                index = across * s.n_rcv + behind
                 owner = lax.rem(rcv + s.n_rcv - behind, s.n_rcv)
-                place = (src ^ across) * s.n_rcv + owner
+                place = (src ^ mask) * s.n_rcv + owner
+                block = filtered[2 * odd_mask + half].at[at, behind]
                 copies.append(
-                    pltpu.make_async_copy(filtered[index], right.at[place], sems.at[index])
+                    pltpu.make_async_copy(block, right.at[place], sems.at[len(copies)])
                 )
+        for index, block in enumerate(left_blocks):
+            copies.append(
+                pltpu.make_async_copy(block, left_held.at[index], left_sems.at[index])
+            )
         for copy in copies:
             copy.start()
         for copy in copies:
             copy.wait()
         row = lax.broadcasted_iota(jnp.int32, (PANEL, s.depth), 0)
-        lane = lax.broadcasted_iota(jnp.int32, (PANEL, s.depth), 1)
+        lane = lax.broadcasted_iota(jnp.int32, (1, s.depth), 1)
         column, _part = lane_parts(lane % LANES, s)
         column = column + (lane // LANES) * s.panel_cols
         chosen = row == (column % s.halves) * LANES + column // s.halves
         spread = jnp.where(chosen, 1.0, 0.0).astype(BF16)
         held = [right[:, s.slots + h].reshape(s.depth, LANES) for h in range(s.halves)]
         own_columns[...] = dot(jnp.concatenate(held, axis=1), spread).astype(BF16)
-
-    clip = clip_rows[...]
-    clip_squared = clip * clip
-
-    own, before, after = left_blocks[0], left_blocks[1 : s.n_rcv], left_blocks[s.n_rcv :]
-    blocks = []
-    for place in range(s.n_rcv):
-        block = own[...]
-        for at in range(s.n_rcv):
-            if at > place:
-                block = jnp.where(rcv == at, before[at - place - 1][...], block)
-            elif at < place:
-                block = jnp.where(rcv == at, after[place - at - 1][...], block)
-        blocks.append(block.astype(F32))
-    plain = jnp.concatenate(blocks, axis=1)
-    lane = lax.broadcasted_iota(jnp.int32, (tile_rows, s.depth), 1)
-    is_real = (lane // s.own) % 2 == 0
-    swapped = jnp.where(
-        is_real,
-        pltpu.roll(plain, s.depth - s.own, 1),
-        pltpu.roll(plain, s.own, 1),
-    )
-    sign = jnp.where(is_real, 1.0, -1.0)
-    signed = plain * sign
-    left[:tile_rows] = signed.astype(BF16)
-    left[tile_rows : 2 * tile_rows] = swapped.astype(BF16)
-
-    product = dot(left[: 2 * tile_rows], own_columns[...])
-    real, imag = product[:tile_rows], product[tile_rows:]
-    limiter = limited(real, imag, clip, clip_squared)
-    real, imag = real * limiter, imag * limiter
-    left[2 * tile_rows : 3 * tile_rows] = (signed - jnp.where(is_real, real, -imag)).astype(BF16)
-    left[3 * tile_rows :] = (swapped - jnp.where(is_real, imag, real)).astype(BF16)
-
-    for tile in range(s.slots // tile_slots):
-        place = slice(tile * width, (tile + 1) * width)
-        slots = range(tile * tile_slots, (tile + 1) * tile_slots)
-        pieces = [right[:, slot].reshape(s.depth, LANES) for slot in slots]
-        product = dot(left[...], jnp.concatenate(pieces, axis=1))
-        base_real = recorded[0, :, place].astype(F32)
-        base_imag = recorded[1, :, place].astype(F32)
-        for which, out in enumerate((out_first, out_second)):
-            first = 2 * which * tile_rows
-            real = product[first : first + tile_rows]
-            imag = product[first + tile_rows : first + 2 * tile_rows]
-            limiter = limited(real, imag, clip, clip_squared)
-            out[0, :, place] = (base_real - real * limiter).astype(BF16)
-            out[1, :, place] = (base_imag - imag * limiter).astype(BF16)
+        fill(0, even)
+
+    def products(left, offset):
+        rows = slice(offset, offset + tile_rows)
+        clip = clip_rows[pl.ds(pl.multiple_of(step * 2 * tile_rows + offset, tile_rows), tile_rows), :]
+        clip_squared = clip * clip
+        for tile in range(s.slots // tile_slots):
+            place = slice(tile * width, (tile + 1) * width)
+            spots = range(tile * tile_slots, (tile + 1) * tile_slots)
+            pieces = [right[:, spot].reshape(s.depth, LANES) for spot in spots]
+            joined = jnp.concatenate(pieces, axis=1)
+            base_real = recorded[0, rows, place].astype(F32)
+            base_imag = recorded[1, rows, place].astype(F32)
+            for which, out in enumerate((out_first, out_second)):
+                first = 2 * which * tile_rows
+                product = dot(left[first : first + 2 * tile_rows], joined)
+                real, imag = product[:tile_rows], product[tile_rows:]
+                limiter = limited(real, imag, clip, clip_squared)
+                out[0, rows, place] = (base_real - real * limiter).astype(BF16)
+                out[1, rows, place] = (base_imag - imag * limiter).astype(BF16)
+
+    fill(2 * step + 1, odd)
+    products(even, 0)
+    fill(jnp.minimum(2 * step + 2, 2 * steps - 1), even)
+    products(odd, tile_rows)
 
 
 def update(recorded, clip_level, left_blocks, filtered, s):
-    tile_rows, tile_slots = 128, 2
-    block = pl.BlockSpec((2, tile_rows, s.cols), lambda i: (0, i, 0))
-    left_block = pl.BlockSpec((tile_rows, LANES), lambda i: (i, 0))
+    tile_rows, tile_slots = ROW_BLOCK // 2, 2
     places = s.n_src * s.n_rcv
-    product_flops = 16 * s.rows * s.cols * PANEL
+    anywhere = pl.BlockSpec(memory_space=pl.ANY)
+    block = pl.BlockSpec((2, 2 * tile_rows, s.cols), lambda i: (0, i, 0))
     return pl.pallas_call(
         functools.partial(update_kernel, s, tile_rows, tile_slots),
-        grid=(s.rows // tile_rows,),
-        in_specs=[block, pl.BlockSpec((tile_rows, 1), lambda i: (i, 0))]
-        + [left_block] * len(left_blocks)
-        + [pl.BlockSpec(memory_space=pl.ANY)] * places,
+        grid=(s.rows // (2 * tile_rows),),
+        in_specs=[block, pl.BlockSpec(memory_space=pltpu.VMEM)]
+        + [anywhere] * (len(left_blocks) + len(filtered)),
         out_specs=[block, block],
         out_shape=[jax.ShapeDtypeStruct(recorded.shape, BF16)] * 2,
         scratch_shapes=[
             pltpu.VMEM((places, s.slots + s.halves, 2 * s.own, LANES), BF16),
             pltpu.VMEM((s.depth, s.depth), BF16),
             pltpu.VMEM((4 * tile_rows, s.depth), BF16),
+            pltpu.VMEM((4 * tile_rows, s.depth), BF16),
             pltpu.SemaphoreType.DMA((places,)),
+            pltpu.SemaphoreType.DMA((len(left_blocks),)),
+            pltpu.VMEM((len(left_blocks), s.rows, LANES), BF16),
         ],
         compiler_params=pltpu.CompilerParams(vmem_limit_bytes=VMEM_BYTES),
         cost_estimate=pl.CostEstimate(
-            flops=product_flops, bytes_accessed=6 * 2 * s.rows * s.cols, transcendentals=0
+            flops=32 * s.rows * s.cols * PANEL,
+            bytes_accessed=12 * s.rows * s.cols,
+            transcendentals=0,
         ),
         name="update",
     )(recorded, clip_level[:, None], *left_blocks, *filtered)
@@ -478,46 +549,52 @@
     return [blocks[0]] + [rotate(blocks[k], k, count) for k in range(1, count)]
 
 
-def gather_line(block, count):
-    up = [(at, at + 1) for at in range(count - 1)]
-    down = [(at + 1, at) for at in range(count - 1)]
-    before, after = [], []
-    up_block = down_block = block
-    for _ in range(count - 1):
-        up_block = lax.ppermute(up_block, "rcv", up)
-        down_block = lax.ppermute(down_block, "rcv", down)
-        before.append(up_block)
-        after.append(down_block)
-    return [block] + before + after
-
-
-def gather_cube(pieces, count):
-    steps = [1 << bit for bit in range(1, count.bit_length() - 1)]
-    half = len(pieces) // 2
-    gathered = {}
-    for order, part in ((steps, range(half)), (steps[::-1], range(half, len(pieces)))):
-        for which in part:
-            held = {0: pieces[which]}
-            for step in order:
-                pairs = [(at, at ^ step) for at in range(count)]
-                held.update(
-                    {d ^ step: lax.ppermute(p, "src", pairs) for d, p in sorted(held.items())}
-                )
-            pairs = [(at, at ^ 1) for at in range(count)]
-            held.update({d ^ 1: lax.ppermute(p, "src", pairs) for d, p in sorted(held.items())})
-            for d, p in held.items():
-                gathered[d, which] = p
-    return [gathered[d, which] for d in range(count) for which in range(len(pieces))]
+def route(at, place, count):
+    if count != 4:
+        return (at - place) % count
+    return {0: 0, 1: 1, 2: 2, 3: 4}[at ^ place] if at ^ place != 3 or abs(at - place) == 3 else 3
+
+
+def gather_both(block, pieces, s):
+    def swap(held, axis, count, step):
+        return lax.ppermute(held, axis, [(at, at ^ step) for at in range(count)])
+
+    line = s.n_rcv == 4
+    if line:
+        far, outer = swap(block, "rcv", 4, 2), swap(block, "rcv", 4, 1)
+        left = (far, outer)
+    else:
+        left = tuple(exchange([block] * s.n_rcv, s.n_rcv)[1:])
+    chips = {step: swap(pieces, "src", s.n_src, step) for step in range(2, s.n_src, 2)}
+    block, left, chips, pieces = lax.optimization_barrier((block, left, chips, pieces))
+    chips[0] = pieces
+    if line:
+        far, outer = left
+        ends = lax.ppermute(far, "rcv", [(1, 0), (2, 3)])
+        middle = lax.ppermute(block, "rcv", [(1, 2), (2, 1)])
+        left = (outer, far, middle, ends)
+    count = s.n_src // 2
+    halves = [range(0, count // 2), range(count // 2, count)]
+    same = [jnp.stack([chips[2 * at] for at in half]) for half in halves]
+    other = [swap(half, "src", s.n_src, 1) for half in same]
+    return (block,) + left, same + other
 
 
 def per_device(recorded, obliquity, clip_level):
     s = Sizes(recorded, lax.axis_size("src"), lax.axis_size("rcv"))
     if not s.fits():
         return plain_device(recorded, obliquity, clip_level)
-    moved = exchange(pick_rows(recorded, s), s.n_rcv)
-    left_blocks = gather_line(pick_columns(recorded, s), s.n_rcv)
-    returned = exchange(filter_rows(moved, obliquity, s), s.n_rcv)
-    filtered = gather_cube(returned, s.n_src)
+    blocks = s.rows // PICK_ROWS
+    picked_rows = pick_rows(recorded, s)
+    moved = exchange(picked_rows, s.n_rcv)
+    early = pick_columns(recorded, 0, EARLY, s.cols // 4, picked_rows[0], s)
+    rows = filter_rows(moved, obliquity, early, s)[0]
+    returned = exchange(rows, s.n_rcv)
+    late = pick_columns(recorded, EARLY, blocks - EARLY, s.cols // 8, rows[0], s)
+    pieces, columns = lax.optimization_barrier(
+        (jnp.stack(returned), jnp.concatenate([early, late]))
+    )
+    left_blocks, filtered = gather_both(columns, pieces, s)
     return update(recorded, clip_level, left_blocks, filtered, s)
 
 

time: 172 us -> 149 us (0.87)
  starting transfers between devices: 49.8 us -> 20.4 us
  waiting for transfers between devices: 29.4 us -> 37.2 us
  local copies, waits for them, and re-layouts: 6.48 us -> 3.47 us
    ppermute x34 -> x9, starting transfers between devices: 38.9 us -> 8.36 us  [the longest x7 6.2 us: swap(): return lax.ppermute(held, axis, [(at, at ^ step) for at in range(count)])]
    ppermute x34 -> x9, waiting for transfers between devices: 22.5 us -> 36.2 us  [the longest x7 22.5 us: swap(): return lax.ppermute(held, axis, [(at, at ^ step) for at in range(count)])]
    ppermute x6, waiting for transfers between devices: 6.87 us -> 1.05 us  [rotate(): return lax.ppermute(block, 'rcv', pairs)]
    pallas_call x2 -> x3, Pallas kernels: 21.9 us -> 26 us  [the longest x2 21 us: pick_columns(): pl.pallas_call(functools.partial(pick_columns_kernel, s, chunk), grid=(s....]
    pallas_call x1, Pallas kernels: 57.9 us -> 54.8 us  [update(): pl.pallas_call(functools.partial(update_kernel, s, tile_rows, tile_slots)...]
    reshape x2 -> x0, local copies, waits for them, and re-layouts: 2.37 us -> none  [filter_rows(): weights = jnp.transpose(jnp.transpose(obliquity).reshape(LANES, s.points))]
  transfers between devices with their start and end apart: 40 -> 15, of which waited for: 15 -> 4; matrix products, arithmetic and copies ran while one was open for 3% -> 2% of each run, Pallas kernels for 13% -> 14%
where the time goes in v2:
time: 149 us
  Pallas kernels  85.2 us (57%)
  waiting for transfers between devices  37.2 us (25%)
  starting transfers between devices  20.4 us (14%)
  local copies, waits for them, and re-layouts  3.47 us (2%)
    pallas_call x1, Pallas kernels, update(): pl.pallas_call(functools.partial(update_kernel, s, tile_rows, tile_slots)...  54.8 us
    ppermute x7, waiting for transfers between devices, swap(): return lax.ppermute(held, axis, [(at, at ^ step) for at in range(count)])  22.5 us
    pallas_call x2, Pallas kernels, pick_columns(): pl.pallas_call(functools.partial(pick_columns_kernel, s, chunk), grid=(s....  21 us
    ppermute x1, waiting for transfers between devices, gather_both(): ends = lax.ppermute(far, 'rcv', [(1, 0), (2, 3)])  13.7 us
    ppermute x6, starting transfers between devices, rotate(): return lax.ppermute(block, 'rcv', pairs)  12 us
    ppermute x7, starting transfers between devices, swap(): return lax.ppermute(held, axis, [(at, at ^ step) for at in range(count)])  6.2 us
    pallas_call x1, Pallas kernels, filter_rows(): pl.pallas_call(functools.partial(filter_kernel, s), in_specs=[pl.BlockSpe...  4.99 us
    pallas_call x1, Pallas kernels, pick_rows(): pl.pallas_call(functools.partial(pick_rows_kernel, s), in_specs=[pl.Block...  4.43 us
  transfers between devices with their start and end apart: 15, of which 4 were waited for; matrix products, arithmetic and copies ran while one was open for 2% of the time, Pallas kernels for 14%

profile of v2, /device:TPU:0, one launch (start us, length us, event | category | flops | bytes accessed | tf_op | source)
XLA Modules:
  0.0 148.6 jit_solution(10631640632421475106)
XLA Ops:
  0.6 4.4 %pick_rows.1 = (bf16[8,2,32,128]{3,2,1,0:T(8,128)(2,1)}, bf16[8,2,32,128]{3,2,1,0:T(8,128)(2,1)}, bf16[8,2,32,128]{3,2,1,0:T(8,128)(2,1)}, bf16[8,2,32,128]{3,2,1,0:T(8,128)(2,1)}) custom-call(bf16[2,2048,4096]{2,1,0:T(8,128)(2,1)} %refs_0_.1), custom_call_target="tpu_custom_call" | custom-call | tf_op jit(solution)/shard_map/pick_rows/pallas_call | solution.py:105
  5.1 3.1 %collective-permute-start = (bf16[8,2,32,128]{3,2,1,0:T(8,128)(2,1)}, bf16[8,2,32,128]{3,2,1,0:T(8,128)(2,1)S(1)}, u32[]{:S(2)}, u32[]{:S(2)}) collective-permute-start(bf16[8,2,32,128]{3,2,1,0:T(8,128)(2,1)} %get-tuple-element.20), channel_id=1, source_target_pairs={{0,1},{1,2},{2,3},{3,0},{4,5},{5,6},{6,7},{7,4},{8,9},{9,10},{10,1... | collective-permute-start | bytes 393224 | tf_op jit(solution)/shard_map/ppermute | solution.py:545
  8.1 2.6 %collective-permute-start.1 = (bf16[8,2,32,128]{3,2,1,0:T(8,128)(2,1)}, bf16[8,2,32,128]{3,2,1,0:T(8,128)(2,1)S(1)}, u32[]{:S(2)}, u32[]{:S(2)}) collective-permute-start(bf16[8,2,32,128]{3,2,1,0:T(8,128)(2,1)} %get-tuple-element.21), channel_id=1, source_target_pairs={{0,2},{1,3},{2,0},{3,1},{4,6},{5,7},{6,4},{7,5},{8,10},{9,11},{10,... | collective-permute-start | bytes 393224 | tf_op jit(solution)/shard_map/ppermute | solution.py:545
  10.7 1.3 collective-permute-start.2
  12.1 6.5 %pick_columns.2.refs_7_ = bf16[512,128]{1,0:T(8,128)(2,1)} custom-call(bf16[2,2048,4096]{2,1,0:T(8,128)(2,1)} %refs_0_.1, bf16[8,2,32,128]{3,2,1,0:T(8,128)(2,1)} %get-tuple-element.19.refs_0_), custom_call_target="tpu_custom_call" | custom-call | flops 2147483648 | bytes 8388608 | tf_op jit(solution)/shard_map/pick_columns/pallas_call | solution.py:144
  18.5 0.0 collective-permute-done.refs_1_
  18.5 1.0 collective-permute-done.1.refs_2_
  19.6 0.0 collective-permute-done.2.refs_3_
  19.6 0.0 copy-done.5
  19.6 0.6 copy-done.6
  20.2 0.6 copy-done.7
  20.9 5.0 %filter_rows.1 = (bf16[34,16,128]{2,1,0:T(8,128)(2,1)}, bf16[34,16,128]{2,1,0:T(8,128)(2,1)}, bf16[34,16,128]{2,1,0:T(8,128)(2,1)}, bf16[34,16,128]{2,1,0:T(8,128)(2,1)}) custom-call(bf16[8,2,32,128]{3,2,1,0:T(8,128)(2,1)} %get-tuple-element.19.refs_0_, bf16[8,2,32,128]{3,2,1,0:T(8,128)(2,1)} %copy-done.5, bf16[8,2,32,128]{3,2,1,0:T(8,128)(2,1)} %copy-done.6, ...), custom_call_target="tpu_custom_call" | custom-call | tf_op jit(solution)/shard_map/filter_rows/pallas_call | solution.py:263
  25.9 2.6 %collective-permute-start.3 = (bf16[34,16,128]{2,1,0:T(8,128)(2,1)}, bf16[34,16,128]{2,1,0:T(8,128)(2,1)S(1)}, u32[]{:S(2)}, u32[]{:S(2)}) collective-permute-start(bf16[34,16,128]{2,1,0:T(8,128)(2,1)} %get-tuple-element.24), channel_id=1, source_target_pairs={{0,1},{1,2},{2,3},{3,0},{4,5},{5,6},{6,7},{7,4},{8,9},{9,10},{10,1... | collective-permute-start | bytes 417800 | tf_op jit(solution)/shard_map/ppermute | solution.py:545
  28.5 2.3 %collective-permute-start.4 = (bf16[34,16,128]{2,1,0:T(8,128)(2,1)}, bf16[34,16,128]{2,1,0:T(8,128)(2,1)S(1)}, u32[]{:S(2)}, u32[]{:S(2)}) collective-permute-start(bf16[34,16,128]{2,1,0:T(8,128)(2,1)} %get-tuple-element.25), channel_id=1, source_target_pairs={{0,2},{1,3},{2,0},{3,1},{4,6},{5,7},{6,4},{7,5},{8,10},{9,11},{10,... | collective-permute-start | bytes 417800 | tf_op jit(solution)/shard_map/ppermute | solution.py:545
  30.8 0.1 collective-permute-start.5
  30.9 14.5 %pick_columns.3 = bf16[1536,128]{1,0:T(8,128)(2,1)} custom-call(bf16[2,2048,4096]{2,1,0:T(8,128)(2,1)} %refs_0_.1, bf16[34,16,128]{2,1,0:T(8,128)(2,1)} %get-tuple-element.23.refs_0_), custom_call_target="tpu_custom_call" | custom-call | flops 6442450944 | bytes 25165824 | tf_op jit(solution)/shard_map/pick_columns/pallas_call | solution.py:144
  45.4 0.0 copy-done
  45.4 1.1 pad_maximum_fusion.3.refs_2_
  46.5 0.0 copy-start.4
  46.5 0.0 collective-permute-done.3
  46.5 0.0 collective-permute-done.4
  46.5 0.0 collective-permute-done.5
  46.5 0.1 pad_maximum_fusion.2
  46.6 2.5 %collective-permute-start.10 = (bf16[4,34,16,128]{3,2,1,0:T(8,128)(2,1)S(1)}, bf16[4,34,16,128]{3,2,1,0:T(8,128)(2,1)S(1)}, u32[]{:S(2)}, u32[]{:S(2)}) collective-permute-start(bf16[4,34,16,128]{3,2,1,0:T(8,128)(2,1)S(1)} %pad_maximum_fusion.2), channel_id=1, source_target_pairs={{0,24},{4,28},{8,16},{12,20},{16,8},{20,12},{24,0},{28,4},{1,25},{... | collective-permute-start | bytes 1671176 | tf_op jit(solution)/shard_map/ppermute | solution.py:560
  49.1 0.5 collective-permute-start.9
  49.6 0.5 collective-permute-start.8
  50.2 1.9 %collective-permute-start.7 = (bf16[2048,128]{1,0:T(8,128)(2,1)S(1)}, bf16[2048,128]{1,0:T(8,128)(2,1)S(1)}, u32[]{:S(2)}, u32[]{:S(2)}) collective-permute-start(bf16[2048,128]{1,0:T(8,128)(2,1)S(1)} %pad_maximum_fusion.3.refs_2_), channel_id=1, source_target_pairs={{0,1},{1,0},{2,3},{3,2},{4,5},{5,4},{6,7},{7,6},{8,9},{9,8},{10,11... | collective-permute-start | bytes 1572872 | tf_op jit(solution)/shard_map/ppermute | solution.py:560
  52.1 0.6 collective-permute-start.6
  52.7 19.9 %collective-permute-done.7.refs_3_ = bf16[2048,128]{1,0:T(8,128)(2,1)S(1)} collective-permute-done((bf16[2048,128]{1,0:T(8,128)(2,1)S(1)}, bf16[2048,128]{1,0:T(8,128)(2,1)S(1)}, u32[]{:S(2)}, u32[]{:S(2)}) %collective-permute-start.7) | collective-permute-done | bytes 524320 | tf_op jit(solution)/shard_map/ppermute | solution.py:560
  72.7 2.5 %collective-permute-done.6.refs_4_ = bf16[2048,128]{1,0:T(8,128)(2,1)} collective-permute-done((bf16[2048,128]{1,0:T(8,128)(2,1)S(1)}, bf16[2048,128]{1,0:T(8,128)(2,1)}, u32[]{:S(2)}, u32[]{:S(2)}) %collective-permute-start.6) | collective-permute-done | bytes 524320 | tf_op jit(solution)/shard_map/ppermute | solution.py:560
  75.2 0.0 collective-permute-done.10
  75.2 0.0 collective-permute-done.9
  75.2 0.0 collective-permute-done.8
  75.2 0.1 pad_maximum_fusion.1.refs_8_
  75.4 0.1 collective-permute-start.14
  75.4 0.0 copy-start.8
  75.5 0.1 pad_maximum_fusion.refs_7_
  75.6 0.8 copy-done.1
  76.3 0.0 collective-permute-start.13
  76.3 0.7 collective-permute-start.11
  77.0 1.5 collective-permute-start.12
  78.5 0.0 copy-done.8
  78.5 1.4 copy.7.refs_1_
  79.9 0.0 collective-permute-done.11.refs_5_
  79.9 13.7 %collective-permute-done.12.refs_6_ = bf16[2048,128]{1,0:T(8,128)(2,1)} collective-permute-done((bf16[2048,128]{1,0:T(8,128)(2,1)}, bf16[2048,128]{1,0:T(8,128)(2,1)}, u32[]{:S(2)}, u32[]{:S(2)}) %collective-permute-start.12) | collective-permute-done | bytes 524320 | tf_op jit(solution)/shard_map/ppermute | solution.py:573
  93.6 0.0 collective-permute-done.14.refs_10_
  93.6 0.0 collective-permute-done.13.refs_9_
  93.6 54.8 %update.1 = (bf16[2,2048,4096]{2,1,0:T(8,128)(2,1)}, bf16[2,2048,4096]{2,1,0:T(8,128)(2,1)}) custom-call(bf16[2,2048,4096]{2,1,0:T(8,128)(2,1)} %refs_0_.1, f32[2048,1]{1,0:T(8,128)} %copy.7.refs_1_, bf16[2048,128]{1,0:T(8,128)(2,1)} %copy-done.4, bf16[2048,128]{1,0:T(8,128)(2,1)} %copy-done.9, bf16[2048,128]{1,0:T(8,128)(2,1)} %collective-permute-done.6.refs_4_, ...), custom_call_target="tpu_custom_call" | custom-call | flops 68719476736 | bytes 100663296 | tf_op jit(solution)/shard_map/update/pallas_call | solution.py:517
  (14 shorter events, 0.0 us)
Async XLA Ops:
  5.1 13.5 %collective-permute-start = (bf16[8,2,32,128]{3,2,1,0:T(8,128)(2,1)}, bf16[8,2,32,128]{3,2,1,0:T(8,128)(2,1)S(1)}, u32[]{:S(2)}, u32[]{:S(2)}) collective-permute-start(bf16[8,2,32,128]{3,2,1,0:T(8,128)(2,1)} %get-tuple-element.20), channel_id=1, source_target_pairs={{0,1},{1,2},{2,3},{3,0},{4,5},{5,6},{6,7},{7,4},{8,9},{9,10},{10,1... | collective-permute-start | bytes 393224 | tf_op jit(solution)/shard_map/ppermute | solution.py:545
  8.1 11.4 %collective-permute-start.1 = (bf16[8,2,32,128]{3,2,1,0:T(8,128)(2,1)}, bf16[8,2,32,128]{3,2,1,0:T(8,128)(2,1)S(1)}, u32[]{:S(2)}, u32[]{:S(2)}) collective-permute-start(bf16[8,2,32,128]{3,2,1,0:T(8,128)(2,1)} %get-tuple-element.21), channel_id=1, source_target_pairs={{0,2},{1,3},{2,0},{3,1},{4,6},{5,7},{6,4},{7,5},{8,10},{9,11},{10,... | collective-permute-start | bytes 393224 | tf_op jit(solution)/shard_map/ppermute | solution.py:545
  10.7 8.9 %collective-permute-start.2 = (bf16[8,2,32,128]{3,2,1,0:T(8,128)(2,1)}, bf16[8,2,32,128]{3,2,1,0:T(8,128)(2,1)S(1)}, u32[]{:S(2)}, u32[]{:S(2)}) collective-permute-start(bf16[8,2,32,128]{3,2,1,0:T(8,128)(2,1)} %get-tuple-element.22), channel_id=1, source_target_pairs={{0,3},{1,0},{2,1},{3,2},{4,7},{5,4},{6,5},{7,6},{8,11},{9,8},{10,9... | collective-permute-start | bytes 393224 | tf_op jit(solution)/shard_map/ppermute | solution.py:545
  18.5 1.1 copy-start.5
  19.6 0.7 copy-start.6
  20.2 0.7 copy-start.7
  25.9 20.6 %collective-permute-start.3 = (bf16[34,16,128]{2,1,0:T(8,128)(2,1)}, bf16[34,16,128]{2,1,0:T(8,128)(2,1)S(1)}, u32[]{:S(2)}, u32[]{:S(2)}) collective-permute-start(bf16[34,16,128]{2,1,0:T(8,128)(2,1)} %get-tuple-element.24), channel_id=1, source_target_pairs={{0,1},{1,2},{2,3},{3,0},{4,5},{5,6},{6,7},{7,4},{8,9},{9,10},{10,1... | collective-permute-start | bytes 417800 | tf_op jit(solution)/shard_map/ppermute | solution.py:545
  28.5 18.0 %collective-permute-start.4 = (bf16[34,16,128]{2,1,0:T(8,128)(2,1)}, bf16[34,16,128]{2,1,0:T(8,128)(2,1)S(1)}, u32[]{:S(2)}, u32[]{:S(2)}) collective-permute-start(bf16[34,16,128]{2,1,0:T(8,128)(2,1)} %get-tuple-element.25), channel_id=1, source_target_pairs={{0,2},{1,3},{2,0},{3,1},{4,6},{5,7},{6,4},{7,5},{8,10},{9,11},{10,... | collective-permute-start | bytes 417800 | tf_op jit(solution)/shard_map/ppermute | solution.py:545
  30.8 15.7 %collective-permute-start.5 = (bf16[34,16,128]{2,1,0:T(8,128)(2,1)}, bf16[34,16,128]{2,1,0:T(8,128)(2,1)S(1)}, u32[]{:S(2)}, u32[]{:S(2)}) collective-permute-start(bf16[34,16,128]{2,1,0:T(8,128)(2,1)} %get-tuple-element.26), channel_id=1, source_target_pairs={{0,3},{1,0},{2,1},{3,2},{4,7},{5,4},{6,5},{7,6},{8,11},{9,8},{10,9... | collective-permute-start | bytes 417800 | tf_op jit(solution)/shard_map/ppermute | solution.py:545
  30.9 14.5 %copy-start = (bf16[512,128]{1,0:T(8,128)(2,1)S(1)}, bf16[512,128]{1,0:T(8,128)(2,1)}, u32[]{:S(2)}) copy-start(bf16[512,128]{1,0:T(8,128)(2,1)} %pick_columns.2.refs_7_) | copy-start | bytes 393220
  45.4 1.1 copy-start.3
  46.5 29.9 %copy-start.4 = (bf16[2048,128]{1,0:T(8,128)(2,1)}, bf16[2048,128]{1,0:T(8,128)(2,1)S(1)}, u32[]{:S(2)}) copy-start(bf16[2048,128]{1,0:T(8,128)(2,1)S(1)} %pad_maximum_fusion.3.refs_2_) | copy-start | bytes 1572868
  46.6 28.6 %collective-permute-start.10 = (bf16[4,34,16,128]{3,2,1,0:T(8,128)(2,1)S(1)}, bf16[4,34,16,128]{3,2,1,0:T(8,128)(2,1)S(1)}, u32[]{:S(2)}, u32[]{:S(2)}) collective-permute-start(bf16[4,34,16,128]{3,2,1,0:T(8,128)(2,1)S(1)} %pad_maximum_fusion.2), channel_id=1, source_target_pairs={{0,24},{4,28},{8,16},{12,20},{16,8},{20,12},{24,0},{28,4},{1,25},{... | collective-permute-start | bytes 1671176 | tf_op jit(solution)/shard_map/ppermute | solution.py:560
  49.1 26.1 %collective-permute-start.9 = (bf16[4,34,16,128]{3,2,1,0:T(8,128)(2,1)S(1)}, bf16[4,34,16,128]{3,2,1,0:T(8,128)(2,1)S(1)}, u32[]{:S(2)}, u32[]{:S(2)}) collective-permute-start(bf16[4,34,16,128]{3,2,1,0:T(8,128)(2,1)S(1)} %pad_maximum_fusion.2), channel_id=1, source_target_pairs={{0,16},{4,20},{8,24},{12,28},{16,0},{20,4},{24,8},{28,12},{1,17},{... | collective-permute-start | bytes 1671176 | tf_op jit(solution)/shard_map/ppermute | solution.py:560
  49.6 25.6 %collective-permute-start.8 = (bf16[4,34,16,128]{3,2,1,0:T(8,128)(2,1)S(1)}, bf16[4,34,16,128]{3,2,1,0:T(8,128)(2,1)S(1)}, u32[]{:S(2)}, u32[]{:S(2)}) collective-permute-start(bf16[4,34,16,128]{3,2,1,0:T(8,128)(2,1)S(1)} %pad_maximum_fusion.2), channel_id=1, source_target_pairs={{0,8},{4,12},{8,0},{12,4},{16,24},{20,28},{24,16},{28,20},{1,9},{5... | collective-permute-start | bytes 1671176 | tf_op jit(solution)/shard_map/ppermute | solution.py:560
  50.2 22.5 %collective-permute-start.7 = (bf16[2048,128]{1,0:T(8,128)(2,1)S(1)}, bf16[2048,128]{1,0:T(8,128)(2,1)S(1)}, u32[]{:S(2)}, u32[]{:S(2)}) collective-permute-start(bf16[2048,128]{1,0:T(8,128)(2,1)S(1)} %pad_maximum_fusion.3.refs_2_), channel_id=1, source_target_pairs={{0,1},{1,0},{2,3},{3,2},{4,5},{5,4},{6,7},{7,6},{8,9},{9,8},{10,11... | collective-permute-start | bytes 1572872 | tf_op jit(solution)/shard_map/ppermute | solution.py:560
  52.1 23.1 %collective-permute-start.6 = (bf16[2048,128]{1,0:T(8,128)(2,1)S(1)}, bf16[2048,128]{1,0:T(8,128)(2,1)}, u32[]{:S(2)}, u32[]{:S(2)}) collective-permute-start(bf16[2048,128]{1,0:T(8,128)(2,1)S(1)} %pad_maximum_fusion.3.refs_2_), channel_id=1, source_target_pairs={{0,2},{1,3},{2,0},{3,1},{4,6},{5,7},{6,4},{7,5},{8,10},{9,11},{10,... | collective-permute-start | bytes 1572872 | tf_op jit(solution)/shard_map/ppermute | solution.py:560
  72.7 2.7 %copy-start.9 = (bf16[2048,128]{1,0:T(8,128)(2,1)}, bf16[2048,128]{1,0:T(8,128)(2,1)S(1)}, u32[]{:S(2)}) copy-start(bf16[2048,128]{1,0:T(8,128)(2,1)S(1)} %collective-permute-done.7.refs_3_) | copy-start | bytes 1572868
  75.4 1.0 copy-start.1
  75.4 18.2 %collective-permute-start.14 = (bf16[2,4,34,16,128]{4,3,2,1,0:T(8,128)(2,1)S(1)}, bf16[2,4,34,16,128]{4,3,2,1,0:T(8,128)(2,1)}, u32[]{:S(2)}, u32[]{:S(2)}) collective-permute-start(bf16[2,4,34,16,128]{4,3,2,1,0:T(8,128)(2,1)S(1)} %pad_maximum_fusion.1.refs_8_), channel_id=1, source_target_pairs={{0,4},{4,0},{8,12},{12,8},{16,20},{20,16},{24,28},{28,24},{1,5},{5... | collective-permute-start | bytes 3342344 | tf_op jit(solution)/shard_map/ppermute | solution.py:560
  75.4 3.1 %copy-start.8 = (f32[2048]{0:T(1024)S(1)}, f32[2048]{0:T(1024)}, u32[]{:S(2)}) copy-start(f32[2048]{0:T(1024)} %param.7) | copy-start | bytes 24580
  76.3 17.3 %copy-start.2 = (bf16[2,4,34,16,128]{4,3,2,1,0:T(8,128)(2,1)}, bf16[2,4,34,16,128]{4,3,2,1,0:T(8,128)(2,1)S(1)}, u32[]{:S(2)}) copy-start(bf16[2,4,34,16,128]{4,3,2,1,0:T(8,128)(2,1)S(1)} %pad_maximum_fusion.refs_7_) | copy-start | bytes 3342340
  76.3 17.2 %collective-permute-start.13 = (bf16[2,4,34,16,128]{4,3,2,1,0:T(8,128)(2,1)S(1)}, bf16[2,4,34,16,128]{4,3,2,1,0:T(8,128)(2,1)}, u32[]{:S(2)}, u32[]{:S(2)}) collective-permute-start(bf16[2,4,34,16,128]{4,3,2,1,0:T(8,128)(2,1)S(1)} %pad_maximum_fusion.refs_7_), channel_id=1, source_target_pairs={{0,4},{4,0},{8,12},{12,8},{16,20},{20,16},{24,28},{28,24},{1,5},{5... | collective-permute-start | bytes 3342344 | tf_op jit(solution)/shard_map/ppermute | solution.py:560
  76.3 3.6 %collective-permute-start.11 = (bf16[2048,128]{1,0:T(8,128)(2,1)S(1)}, bf16[2048,128]{1,0:T(8,128)(2,1)S(1)}, u32[]{:S(2)}, u32[]{:S(2)}) collective-permute-start(bf16[2048,128]{1,0:T(8,128)(2,1)S(1)} %pad_maximum_fusion.3.refs_2_), channel_id=1, source_target_pairs={{1,2},{2,1},{5,6},{6,5},{9,10},{10,9},{13,14},{14,13},{17,18},{18,... | collective-permute-start | bytes 1572872 | tf_op jit(solution)/shard_map/ppermute | solution.py:574
  77.0 16.5 %collective-permute-start.12 = (bf16[2048,128]{1,0:T(8,128)(2,1)}, bf16[2048,128]{1,0:T(8,128)(2,1)}, u32[]{:S(2)}, u32[]{:S(2)}) collective-permute-start(bf16[2048,128]{1,0:T(8,128)(2,1)} %collective-permute-done.6.refs_4_), channel_id=1, source_target_pairs={{1,0},{2,3},{5,4},{6,7},{9,8},{10,11},{13,12},{14,15},{17,16},{18,... | collective-permute-start | bytes 1572872 | tf_op jit(solution)/shard_map/ppermute | solution.py:573
  79.9 13.7 %copy-start.10 = (bf16[2048,128]{1,0:T(8,128)(2,1)}, bf16[2048,128]{1,0:T(8,128)(2,1)S(1)}, u32[]{:S(2)}) copy-start(bf16[2048,128]{1,0:T(8,128)(2,1)S(1)} %collective-permute-done.11.refs_5_) | copy-start | bytes 1572868

commit v3 on v2

--- a/solution.py
+++ b/solution.py
@@ -587,10 +587,10 @@
     blocks = s.rows // PICK_ROWS
     picked_rows = pick_rows(recorded, s)
     moved = exchange(picked_rows, s.n_rcv)
-    early = pick_columns(recorded, 0, EARLY, s.cols // 4, picked_rows[0], s)
+    early = pick_columns(recorded, 0, EARLY, s.cols // 2, picked_rows[0], s)
     rows = filter_rows(moved, obliquity, early, s)[0]
     returned = exchange(rows, s.n_rcv)
-    late = pick_columns(recorded, EARLY, blocks - EARLY, s.cols // 8, rows[0], s)
+    late = pick_columns(recorded, EARLY, blocks - EARLY, s.cols // 4, rows[0], s)
     pieces, columns = lax.optimization_barrier(
         (jnp.stack(returned), jnp.concatenate([early, late]))
     )

time: 149 us -> 147 us (0.987)
  Pallas kernels: 85.2 us -> 82.4 us
    pallas_call x2, Pallas kernels: 21 us -> 18.2 us  [pick_columns(): pl.pallas_call(functools.partial(pick_columns_kernel, s, chunk), grid=(s....]
  transfers between devices with their start and end apart: 15 -> 15, of which waited for: 4 -> 4; matrix products, arithmetic and copies ran while one was open for 2% -> 2% of each run, Pallas kernels for 14% -> 12%
where the time goes in v3:
time: 147 us
  Pallas kernels  82.4 us (56%)
  waiting for transfers between devices  38 us (26%)
  starting transfers between devices  20.4 us (14%)
  local copies, waits for them, and re-layouts  3.47 us (2%)
    pallas_call x1, Pallas kernels, update(): pl.pallas_call(functools.partial(update_kernel, s, tile_rows, tile_slots)...  54.8 us
    ppermute x7, waiting for transfers between devices, swap(): return lax.ppermute(held, axis, [(at, at ^ step) for at in range(count)])  22.5 us
    pallas_call x2, Pallas kernels, pick_columns(): pl.pallas_call(functools.partial(pick_columns_kernel, s, chunk), grid=(s....  18.2 us
    ppermute x1, waiting for transfers between devices, gather_both(): ends = lax.ppermute(far, 'rcv', [(1, 0), (2, 3)])  13.7 us
    ppermute x6, starting transfers between devices, rotate(): return lax.ppermute(block, 'rcv', pairs)  12 us
    ppermute x7, starting transfers between devices, swap(): return lax.ppermute(held, axis, [(at, at ^ step) for at in range(count)])  6.2 us
    pallas_call x1, Pallas kernels, filter_rows(): pl.pallas_call(functools.partial(filter_kernel, s), in_specs=[pl.BlockSpe...  4.99 us
    pallas_call x1, Pallas kernels, pick_rows(): pl.pallas_call(functools.partial(pick_rows_kernel, s), in_specs=[pl.Block...  4.43 us
  transfers between devices with their start and end apart: 15, of which 4 were waited for; matrix products, arithmetic and copies ran while one was open for 2% of the time, Pallas kernels for 12%

profile of v3, /device:TPU:0, one launch (start us, length us, event | category | flops | bytes accessed | tf_op | source)
XLA Modules:
  0.0 146.6 jit_solution(9599165049409686480)
XLA Ops:
  0.6 4.4 %pick_rows.1 = (bf16[8,2,32,128]{3,2,1,0:T(8,128)(2,1)}, bf16[8,2,32,128]{3,2,1,0:T(8,128)(2,1)}, bf16[8,2,32,128]{3,2,1,0:T(8,128)(2,1)}, bf16[8,2,32,128]{3,2,1,0:T(8,128)(2,1)}) custom-call(bf16[2,2048,4096]{2,1,0:T(8,128)(2,1)} %refs_0_.1), custom_call_target="tpu_custom_call" | custom-call | tf_op jit(solution)/shard_map/pick_rows/pallas_call | solution.py:105
  5.1 3.1 %collective-permute-start = (bf16[8,2,32,128]{3,2,1,0:T(8,128)(2,1)}, bf16[8,2,32,128]{3,2,1,0:T(8,128)(2,1)S(1)}, u32[]{:S(2)}, u32[]{:S(2)}) collective-permute-start(bf16[8,2,32,128]{3,2,1,0:T(8,128)(2,1)} %get-tuple-element.20), channel_id=1, source_target_pairs={{0,1},{1,2},{2,3},{3,0},{4,5},{5,6},{6,7},{7,4},{8,9},{9,10},{10,1... | collective-permute-start | bytes 393224 | tf_op jit(solution)/shard_map/ppermute | solution.py:545
  8.1 2.6 %collective-permute-start.1 = (bf16[8,2,32,128]{3,2,1,0:T(8,128)(2,1)}, bf16[8,2,32,128]{3,2,1,0:T(8,128)(2,1)S(1)}, u32[]{:S(2)}, u32[]{:S(2)}) collective-permute-start(bf16[8,2,32,128]{3,2,1,0:T(8,128)(2,1)} %get-tuple-element.21), channel_id=1, source_target_pairs={{0,2},{1,3},{2,0},{3,1},{4,6},{5,7},{6,4},{7,5},{8,10},{9,11},{10,... | collective-permute-start | bytes 393224 | tf_op jit(solution)/shard_map/ppermute | solution.py:545
  10.7 1.3 collective-permute-start.2
  12.1 5.6 %pick_columns.2.refs_7_ = bf16[512,128]{1,0:T(8,128)(2,1)} custom-call(bf16[2,2048,4096]{2,1,0:T(8,128)(2,1)} %refs_0_.1, bf16[8,2,32,128]{3,2,1,0:T(8,128)(2,1)} %get-tuple-element.19.refs_0_), custom_call_target="tpu_custom_call" | custom-call | flops 2147483648 | bytes 8388608 | tf_op jit(solution)/shard_map/pick_columns/pallas_call | solution.py:144
  17.7 0.0 collective-permute-done.refs_1_
  17.7 1.9 %collective-permute-done.1.refs_2_ = bf16[8,2,32,128]{3,2,1,0:T(8,128)(2,1)S(1)} collective-permute-done((bf16[8,2,32,128]{3,2,1,0:T(8,128)(2,1)}, bf16[8,2,32,128]{3,2,1,0:T(8,128)(2,1)S(1)}, u32[]{:S(2)}, u32[]{:S(2)}) %collective-permute-start.1) | collective-permute-done | bytes 131104 | tf_op jit(solution)/shard_map/ppermute | solution.py:545
  19.6 0.0 collective-permute-done.2.refs_3_
  19.6 0.0 copy-done.5
  19.6 0.6 copy-done.6
  20.2 0.6 copy-done.7
  20.9 5.0 %filter_rows.1 = (bf16[34,16,128]{2,1,0:T(8,128)(2,1)}, bf16[34,16,128]{2,1,0:T(8,128)(2,1)}, bf16[34,16,128]{2,1,0:T(8,128)(2,1)}, bf16[34,16,128]{2,1,0:T(8,128)(2,1)}) custom-call(bf16[8,2,32,128]{3,2,1,0:T(8,128)(2,1)} %get-tuple-element.19.refs_0_, bf16[8,2,32,128]{3,2,1,0:T(8,128)(2,1)} %copy-done.5, bf16[8,2,32,128]{3,2,1,0:T(8,128)(2,1)} %copy-done.6, ...), custom_call_target="tpu_custom_call" | custom-call | tf_op jit(solution)/shard_map/filter_rows/pallas_call | solution.py:263
  25.9 2.6 %collective-permute-start.3 = (bf16[34,16,128]{2,1,0:T(8,128)(2,1)}, bf16[34,16,128]{2,1,0:T(8,128)(2,1)S(1)}, u32[]{:S(2)}, u32[]{:S(2)}) collective-permute-start(bf16[34,16,128]{2,1,0:T(8,128)(2,1)} %get-tuple-element.24), channel_id=1, source_target_pairs={{0,1},{1,2},{2,3},{3,0},{4,5},{5,6},{6,7},{7,4},{8,9},{9,10},{10,1... | collective-permute-start | bytes 417800 | tf_op jit(solution)/shard_map/ppermute | solution.py:545
  28.5 2.3 %collective-permute-start.4 = (bf16[34,16,128]{2,1,0:T(8,128)(2,1)}, bf16[34,16,128]{2,1,0:T(8,128)(2,1)S(1)}, u32[]{:S(2)}, u32[]{:S(2)}) collective-permute-start(bf16[34,16,128]{2,1,0:T(8,128)(2,1)} %get-tuple-element.25), channel_id=1, source_target_pairs={{0,2},{1,3},{2,0},{3,1},{4,6},{5,7},{6,4},{7,5},{8,10},{9,11},{10,... | collective-permute-start | bytes 417800 | tf_op jit(solution)/shard_map/ppermute | solution.py:545
  30.8 0.1 collective-permute-start.5
  30.9 12.5 %pick_columns.3 = bf16[1536,128]{1,0:T(8,128)(2,1)} custom-call(bf16[2,2048,4096]{2,1,0:T(8,128)(2,1)} %refs_0_.1, bf16[34,16,128]{2,1,0:T(8,128)(2,1)} %get-tuple-element.23.refs_0_), custom_call_target="tpu_custom_call" | custom-call | flops 6442450944 | bytes 25165824 | tf_op jit(solution)/shard_map/pick_columns/pallas_call | solution.py:144
  43.4 0.0 copy-done
  43.4 1.1 pad_maximum_fusion.3.refs_2_
  44.5 0.0 copy-start.4
  44.5 0.0 collective-permute-done.3
  44.5 0.0 collective-permute-done.4
  44.5 0.0 collective-permute-done.5
  44.5 0.1 pad_maximum_fusion.2
  44.6 2.5 %collective-permute-start.10 = (bf16[4,34,16,128]{3,2,1,0:T(8,128)(2,1)S(1)}, bf16[4,34,16,128]{3,2,1,0:T(8,128)(2,1)S(1)}, u32[]{:S(2)}, u32[]{:S(2)}) collective-permute-start(bf16[4,34,16,128]{3,2,1,0:T(8,128)(2,1)S(1)} %pad_maximum_fusion.2), channel_id=1, source_target_pairs={{0,24},{4,28},{8,16},{12,20},{16,8},{20,12},{24,0},{28,4},{1,25},{... | collective-permute-start | bytes 1671176 | tf_op jit(solution)/shard_map/ppermute | solution.py:560
  47.1 0.5 collective-permute-start.9
  47.7 0.5 collective-permute-start.8
  48.2 1.9 %collective-permute-start.7 = (bf16[2048,128]{1,0:T(8,128)(2,1)S(1)}, bf16[2048,128]{1,0:T(8,128)(2,1)S(1)}, u32[]{:S(2)}, u32[]{:S(2)}) collective-permute-start(bf16[2048,128]{1,0:T(8,128)(2,1)S(1)} %pad_maximum_fusion.3.refs_2_), channel_id=1, source_target_pairs={{0,1},{1,0},{2,3},{3,2},{4,5},{5,4},{6,7},{7,6},{8,9},{9,8},{10,11... | collective-permute-start | bytes 1572872 | tf_op jit(solution)/shard_map/ppermute | solution.py:560
  50.1 0.7 collective-permute-start.6
  50.8 19.9 %collective-permute-done.7.refs_3_ = bf16[2048,128]{1,0:T(8,128)(2,1)S(1)} collective-permute-done((bf16[2048,128]{1,0:T(8,128)(2,1)S(1)}, bf16[2048,128]{1,0:T(8,128)(2,1)S(1)}, u32[]{:S(2)}, u32[]{:S(2)}) %collective-permute-start.7) | collective-permute-done | bytes 524320 | tf_op jit(solution)/shard_map/ppermute | solution.py:560
  70.7 2.5 %collective-permute-done.6.refs_4_ = bf16[2048,128]{1,0:T(8,128)(2,1)} collective-permute-done((bf16[2048,128]{1,0:T(8,128)(2,1)S(1)}, bf16[2048,128]{1,0:T(8,128)(2,1)}, u32[]{:S(2)}, u32[]{:S(2)}) %collective-permute-start.6) | collective-permute-done | bytes 524320 | tf_op jit(solution)/shard_map/ppermute | solution.py:560
  73.2 0.0 collective-permute-done.10
  73.2 0.0 collective-permute-done.9
  73.2 0.0 collective-permute-done.8
  73.2 0.1 pad_maximum_fusion.1.refs_8_
  73.4 0.1 collective-permute-start.14
  73.5 0.0 copy-start.8
  73.5 0.1 pad_maximum_fusion.refs_7_
  73.6 0.8 copy-done.1
  74.4 0.0 collective-permute-start.13
  74.4 0.0 copy-done.4
  74.4 0.7 collective-permute-start.11
  75.1 1.5 %collective-permute-start.12 = (bf16[2048,128]{1,0:T(8,128)(2,1)}, bf16[2048,128]{1,0:T(8,128)(2,1)}, u32[]{:S(2)}, u32[]{:S(2)}) collective-permute-start(bf16[2048,128]{1,0:T(8,128)(2,1)} %collective-permute-done.6.refs_4_), channel_id=1, source_target_pairs={{1,0},{2,3},{5,4},{6,7},{9,8},{10,11},{13,12},{14,15},{17,16},{18,... | collective-permute-start | bytes 1572872 | tf_op jit(solution)/shard_map/ppermute | solution.py:573
  76.5 1.4 copy.7.refs_1_
  77.9 0.0 collective-permute-done.11.refs_5_
  77.9 13.7 %collective-permute-done.12.refs_6_ = bf16[2048,128]{1,0:T(8,128)(2,1)} collective-permute-done((bf16[2048,128]{1,0:T(8,128)(2,1)}, bf16[2048,128]{1,0:T(8,128)(2,1)}, u32[]{:S(2)}, u32[]{:S(2)}) %collective-permute-start.12) | collective-permute-done | bytes 524320 | tf_op jit(solution)/shard_map/ppermute | solution.py:573
  91.6 0.0 collective-permute-done.14.refs_10_
  91.6 0.0 collective-permute-done.13.refs_9_
  91.6 54.8 %update.1 = (bf16[2,2048,4096]{2,1,0:T(8,128)(2,1)}, bf16[2,2048,4096]{2,1,0:T(8,128)(2,1)}) custom-call(bf16[2,2048,4096]{2,1,0:T(8,128)(2,1)} %refs_0_.1, f32[2048,1]{1,0:T(8,128)} %copy.7.refs_1_, bf16[2048,128]{1,0:T(8,128)(2,1)} %copy-done.4, bf16[2048,128]{1,0:T(8,128)(2,1)} %copy-done.9, bf16[2048,128]{1,0:T(8,128)(2,1)} %collective-permute-done.6.refs_4_, ...), custom_call_target="tpu_custom_call" | custom-call | flops 68719476736 | bytes 100663296 | tf_op jit(solution)/shard_map/update/pallas_call | solution.py:517
  (14 shorter events, 0.0 us)
Async XLA Ops:
  5.1 12.7 %collective-permute-start = (bf16[8,2,32,128]{3,2,1,0:T(8,128)(2,1)}, bf16[8,2,32,128]{3,2,1,0:T(8,128)(2,1)S(1)}, u32[]{:S(2)}, u32[]{:S(2)}) collective-permute-start(bf16[8,2,32,128]{3,2,1,0:T(8,128)(2,1)} %get-tuple-element.20), channel_id=1, source_target_pairs={{0,1},{1,2},{2,3},{3,0},{4,5},{5,6},{6,7},{7,4},{8,9},{9,10},{10,1... | collective-permute-start | bytes 393224 | tf_op jit(solution)/shard_map/ppermute | solution.py:545
  8.1 11.4 %collective-permute-start.1 = (bf16[8,2,32,128]{3,2,1,0:T(8,128)(2,1)}, bf16[8,2,32,128]{3,2,1,0:T(8,128)(2,1)S(1)}, u32[]{:S(2)}, u32[]{:S(2)}) collective-permute-start(bf16[8,2,32,128]{3,2,1,0:T(8,128)(2,1)} %get-tuple-element.21), channel_id=1, source_target_pairs={{0,2},{1,3},{2,0},{3,1},{4,6},{5,7},{6,4},{7,5},{8,10},{9,11},{10,... | collective-permute-start | bytes 393224 | tf_op jit(solution)/shard_map/ppermute | solution.py:545
  10.7 8.9 %collective-permute-start.2 = (bf16[8,2,32,128]{3,2,1,0:T(8,128)(2,1)}, bf16[8,2,32,128]{3,2,1,0:T(8,128)(2,1)S(1)}, u32[]{:S(2)}, u32[]{:S(2)}) collective-permute-start(bf16[8,2,32,128]{3,2,1,0:T(8,128)(2,1)} %get-tuple-element.22), channel_id=1, source_target_pairs={{0,3},{1,0},{2,1},{3,2},{4,7},{5,4},{6,5},{7,6},{8,11},{9,8},{10,9... | collective-permute-start | bytes 393224 | tf_op jit(solution)/shard_map/ppermute | solution.py:545
  17.7 1.9 %copy-start.5 = (bf16[8,2,32,128]{3,2,1,0:T(8,128)(2,1)}, bf16[8,2,32,128]{3,2,1,0:T(8,128)(2,1)S(1)}, u32[]{:S(2)}) copy-start(bf16[8,2,32,128]{3,2,1,0:T(8,128)(2,1)S(1)} %collective-permute-done.refs_1_) | copy-start | bytes 393220
  19.6 0.7 copy-start.6
  20.2 0.7 copy-start.7
  25.9 18.6 %collective-permute-start.3 = (bf16[34,16,128]{2,1,0:T(8,128)(2,1)}, bf16[34,16,128]{2,1,0:T(8,128)(2,1)S(1)}, u32[]{:S(2)}, u32[]{:S(2)}) collective-permute-start(bf16[34,16,128]{2,1,0:T(8,128)(2,1)} %get-tuple-element.24), channel_id=1, source_target_pairs={{0,1},{1,2},{2,3},{3,0},{4,5},{5,6},{6,7},{7,4},{8,9},{9,10},{10,1... | collective-permute-start | bytes 417800 | tf_op jit(solution)/shard_map/ppermute | solution.py:545
  28.5 16.0 %collective-permute-start.4 = (bf16[34,16,128]{2,1,0:T(8,128)(2,1)}, bf16[34,16,128]{2,1,0:T(8,128)(2,1)S(1)}, u32[]{:S(2)}, u32[]{:S(2)}) collective-permute-start(bf16[34,16,128]{2,1,0:T(8,128)(2,1)} %get-tuple-element.25), channel_id=1, source_target_pairs={{0,2},{1,3},{2,0},{3,1},{4,6},{5,7},{6,4},{7,5},{8,10},{9,11},{10,... | collective-permute-start | bytes 417800 | tf_op jit(solution)/shard_map/ppermute | solution.py:545
  30.8 13.7 %collective-permute-start.5 = (bf16[34,16,128]{2,1,0:T(8,128)(2,1)}, bf16[34,16,128]{2,1,0:T(8,128)(2,1)S(1)}, u32[]{:S(2)}, u32[]{:S(2)}) collective-permute-start(bf16[34,16,128]{2,1,0:T(8,128)(2,1)} %get-tuple-element.26), channel_id=1, source_target_pairs={{0,3},{1,0},{2,1},{3,2},{4,7},{5,4},{6,5},{7,6},{8,11},{9,8},{10,9... | collective-permute-start | bytes 417800 | tf_op jit(solution)/shard_map/ppermute | solution.py:545
  30.9 12.5 %copy-start = (bf16[512,128]{1,0:T(8,128)(2,1)S(1)}, bf16[512,128]{1,0:T(8,128)(2,1)}, u32[]{:S(2)}) copy-start(bf16[512,128]{1,0:T(8,128)(2,1)} %pick_columns.2.refs_7_) | copy-start | bytes 393220
  43.4 1.1 copy-start.3
  44.5 29.9 %copy-start.4 = (bf16[2048,128]{1,0:T(8,128)(2,1)}, bf16[2048,128]{1,0:T(8,128)(2,1)S(1)}, u32[]{:S(2)}) copy-start(bf16[2048,128]{1,0:T(8,128)(2,1)S(1)} %pad_maximum_fusion.3.refs_2_) | copy-start | bytes 1572868
  44.6 28.6 %collective-permute-start.10 = (bf16[4,34,16,128]{3,2,1,0:T(8,128)(2,1)S(1)}, bf16[4,34,16,128]{3,2,1,0:T(8,128)(2,1)S(1)}, u32[]{:S(2)}, u32[]{:S(2)}) collective-permute-start(bf16[4,34,16,128]{3,2,1,0:T(8,128)(2,1)S(1)} %pad_maximum_fusion.2), channel_id=1, source_target_pairs={{0,24},{4,28},{8,16},{12,20},{16,8},{20,12},{24,0},{28,4},{1,25},{... | collective-permute-start | bytes 1671176 | tf_op jit(solution)/shard_map/ppermute | solution.py:560
  47.1 26.1 %collective-permute-start.9 = (bf16[4,34,16,128]{3,2,1,0:T(8,128)(2,1)S(1)}, bf16[4,34,16,128]{3,2,1,0:T(8,128)(2,1)S(1)}, u32[]{:S(2)}, u32[]{:S(2)}) collective-permute-start(bf16[4,34,16,128]{3,2,1,0:T(8,128)(2,1)S(1)} %pad_maximum_fusion.2), channel_id=1, source_target_pairs={{0,16},{4,20},{8,24},{12,28},{16,0},{20,4},{24,8},{28,12},{1,17},{... | collective-permute-start | bytes 1671176 | tf_op jit(solution)/shard_map/ppermute | solution.py:560
  47.7 25.6 %collective-permute-start.8 = (bf16[4,34,16,128]{3,2,1,0:T(8,128)(2,1)S(1)}, bf16[4,34,16,128]{3,2,1,0:T(8,128)(2,1)S(1)}, u32[]{:S(2)}, u32[]{:S(2)}) collective-permute-start(bf16[4,34,16,128]{3,2,1,0:T(8,128)(2,1)S(1)} %pad_maximum_fusion.2), channel_id=1, source_target_pairs={{0,8},{4,12},{8,0},{12,4},{16,24},{20,28},{24,16},{28,20},{1,9},{5... | collective-permute-start | bytes 1671176 | tf_op jit(solution)/shard_map/ppermute | solution.py:560
  48.2 22.5 %collective-permute-start.7 = (bf16[2048,128]{1,0:T(8,128)(2,1)S(1)}, bf16[2048,128]{1,0:T(8,128)(2,1)S(1)}, u32[]{:S(2)}, u32[]{:S(2)}) collective-permute-start(bf16[2048,128]{1,0:T(8,128)(2,1)S(1)} %pad_maximum_fusion.3.refs_2_), channel_id=1, source_target_pairs={{0,1},{1,0},{2,3},{3,2},{4,5},{5,4},{6,7},{7,6},{8,9},{9,8},{10,11... | collective-permute-start | bytes 1572872 | tf_op jit(solution)/shard_map/ppermute | solution.py:560
  50.1 23.1 %collective-permute-start.6 = (bf16[2048,128]{1,0:T(8,128)(2,1)S(1)}, bf16[2048,128]{1,0:T(8,128)(2,1)}, u32[]{:S(2)}, u32[]{:S(2)}) collective-permute-start(bf16[2048,128]{1,0:T(8,128)(2,1)S(1)} %pad_maximum_fusion.3.refs_2_), channel_id=1, source_target_pairs={{0,2},{1,3},{2,0},{3,1},{4,6},{5,7},{6,4},{7,5},{8,10},{9,11},{10,... | collective-permute-start | bytes 1572872 | tf_op jit(solution)/shard_map/ppermute | solution.py:560
  70.7 2.7 %copy-start.9 = (bf16[2048,128]{1,0:T(8,128)(2,1)}, bf16[2048,128]{1,0:T(8,128)(2,1)S(1)}, u32[]{:S(2)}) copy-start(bf16[2048,128]{1,0:T(8,128)(2,1)S(1)} %collective-permute-done.7.refs_3_) | copy-start | bytes 1572868
  73.4 1.0 copy-start.1
  73.4 18.2 %collective-permute-start.14 = (bf16[2,4,34,16,128]{4,3,2,1,0:T(8,128)(2,1)S(1)}, bf16[2,4,34,16,128]{4,3,2,1,0:T(8,128)(2,1)}, u32[]{:S(2)}, u32[]{:S(2)}) collective-permute-start(bf16[2,4,34,16,128]{4,3,2,1,0:T(8,128)(2,1)S(1)} %pad_maximum_fusion.1.refs_8_), channel_id=1, source_target_pairs={{0,4},{4,0},{8,12},{12,8},{16,20},{20,16},{24,28},{28,24},{1,5},{5... | collective-permute-start | bytes 3342344 | tf_op jit(solution)/shard_map/ppermute | solution.py:560
  73.5 3.1 %copy-start.8 = (f32[2048]{0:T(1024)S(1)}, f32[2048]{0:T(1024)}, u32[]{:S(2)}) copy-start(f32[2048]{0:T(1024)} %param.7) | copy-start | bytes 24580
  74.3 17.3 %copy-start.2 = (bf16[2,4,34,16,128]{4,3,2,1,0:T(8,128)(2,1)}, bf16[2,4,34,16,128]{4,3,2,1,0:T(8,128)(2,1)S(1)}, u32[]{:S(2)}) copy-start(bf16[2,4,34,16,128]{4,3,2,1,0:T(8,128)(2,1)S(1)} %pad_maximum_fusion.refs_7_) | copy-start | bytes 3342340
  74.4 17.2 %collective-permute-start.13 = (bf16[2,4,34,16,128]{4,3,2,1,0:T(8,128)(2,1)S(1)}, bf16[2,4,34,16,128]{4,3,2,1,0:T(8,128)(2,1)}, u32[]{:S(2)}, u32[]{:S(2)}) collective-permute-start(bf16[2,4,34,16,128]{4,3,2,1,0:T(8,128)(2,1)S(1)} %pad_maximum_fusion.refs_7_), channel_id=1, source_target_pairs={{0,4},{4,0},{8,12},{12,8},{16,20},{20,16},{24,28},{28,24},{1,5},{5... | collective-permute-start | bytes 3342344 | tf_op jit(solution)/shard_map/ppermute | solution.py:560
  74.4 3.6 %collective-permute-start.11 = (bf16[2048,128]{1,0:T(8,128)(2,1)S(1)}, bf16[2048,128]{1,0:T(8,128)(2,1)S(1)}, u32[]{:S(2)}, u32[]{:S(2)}) collective-permute-start(bf16[2048,128]{1,0:T(8,128)(2,1)S(1)} %pad_maximum_fusion.3.refs_2_), channel_id=1, source_target_pairs={{1,2},{2,1},{5,6},{6,5},{9,10},{10,9},{13,14},{14,13},{17,18},{18,... | collective-permute-start | bytes 1572872 | tf_op jit(solution)/shard_map/ppermute | solution.py:574
  75.1 16.5 %collective-permute-start.12 = (bf16[2048,128]{1,0:T(8,128)(2,1)}, bf16[2048,128]{1,0:T(8,128)(2,1)}, u32[]{:S(2)}, u32[]{:S(2)}) collective-permute-start(bf16[2048,128]{1,0:T(8,128)(2,1)} %collective-permute-done.6.refs_4_), channel_id=1, source_target_pairs={{1,0},{2,3},{5,4},{6,7},{9,8},{10,11},{13,12},{14,15},{17,16},{18,... | collective-permute-start | bytes 1572872 | tf_op jit(solution)/shard_map/ppermute | solution.py:573
  77.9 13.7 %copy-start.10 = (bf16[2048,128]{1,0:T(8,128)(2,1)}, bf16[2048,128]{1,0:T(8,128)(2,1)S(1)}, u32[]{:S(2)}) copy-start(bf16[2048,128]{1,0:T(8,128)(2,1)S(1)} %collective-permute-done.11.refs_5_) | copy-start | bytes 1572868
